TPU v7x, 256 devices: a whole 4x4x8 slice. The times are simulated.
256 devices in a mesh: row: 16 (over y, x_lo, core), col: 16 (over z, x_hi).
Axes of the slice: x: 4 (x_hi: 2, x_lo: 2; x = x_hi * 2 + x_lo), y: 4, z: 8, core: 2. Of those that a mesh axis runs over, the one named last changes fastest.
Arguments:
- node_feats: bfloat16 [524288, 128], P(('row', 'col')), may hold values from -6 to 6
- tile_vals: bfloat16 [16, 16, 256, 128, 128], P('row', 'col'), as said below
- tile_dest: int32 [16, 16, 256], P('row', 'col'), may hold values from 0 to 255, as said below
- tile_source: int32 [16, 16, 256], P('row', 'col'), may hold values from 0 to 255, as said below
- tile_count: int32 [16, 16], P('row', 'col'), may hold values from 32 to 256, as said below
- weight: bfloat16 [128, 256], replicated, may hold values from -0.5 to 0.5
- out_bias: float32 [256], replicated, may hold values from -3 to 3
Outputs:
- layer_out: bfloat16 [524288, 256], P(('row', 'col'))
Inputs may be any that keep to these rules, and one draw needn't show every extreme that they name: `tile_count`: busiest device holds exactly 256 live tiles in every draw; the loads follow a power law. `tile_dest`: 0 in slots at or past the device's count. The live tiles of one device touch at most 8 distinct destination blocks among the 16 blocks of each index of col, and some device touches exactly that many in every one of them. `tile_source`: 0 in slots at or past the device's count. `tile_vals`: Nonnegative; slots at or past the device's count hold stale values that are not part of A.
All inputs are finite; a program needn't handle non-finite values.
Results may differ from a plain program's by a relative error of at most 0.0047.
Values may be sent and summed in bfloat16 or wider, within the bound.
No kernel may reach another device: no remote copies, remote signals or barrier semaphores. Data moves between devices by JAX's collectives and lax.ppermute only.
A program may use at most 128 MiB of HBM per device.

v0:
```python
import jax
import jax.numpy as jnp
from jax import lax
from jax.sharding import PartitionSpec as P


def on_device(node_feats, tile_vals, tile_dest, tile_source, tile_count, weight, out_bias):
    tile_set = tile_vals[0, 0]
    dest_ids = tile_dest[0, 0]
    source_ids = tile_source[0, 0]
    live_count = tile_count[0, 0]
    slot_count = tile_set.shape[0]
    tile_size = tile_set.shape[1]
    feat_width = node_feats.shape[1]
    own_blocks = node_feats.shape[0] // tile_size
    col_count = lax.axis_size("col")
    gathered = lax.all_gather(node_feats, "row", axis=0, tiled=True)
    blocks = gathered.reshape(-1, tile_size, feat_width)
    dest_blocks = col_count * own_blocks
    partial_value = jnp.zeros((dest_blocks, tile_size, feat_width), jnp.float32)
    is_live = jnp.arange(slot_count, dtype=jnp.int32) < live_count
    products = jnp.einsum(
        "kij,kjf->kif", tile_set, blocks[source_ids], preferred_element_type=jnp.float32
    )
    products = jnp.where(is_live[:, None, None], products, 0.0)
    partial_value = partial_value.at[dest_ids].add(products)
    summed = lax.psum_scatter(
        partial_value.reshape(-1, feat_width), "col", scatter_dimension=0, tiled=True
    )
    hidden = (
        jnp.dot(summed.astype(jnp.bfloat16), weight, preferred_element_type=jnp.float32) + out_bias
    )
    return jnp.maximum(hidden, 0.0).astype(jnp.bfloat16)


def solution(mesh):
    return jax.shard_map(
        on_device,
        mesh=mesh,
        in_specs=(
            P(("row", "col"), None),
            P("row", "col", None, None, None),
            P("row", "col", None),
            P("row", "col", None),
            P("row", "col"),
            P(),
            P(),
        ),
        out_specs=P(("row", "col"), None),
        check_vma=False,
    )
```

profile of v0, /device:TPU:1, one launch (start us, length us, event | category | flops | bytes accessed | tf_op | source)
XLA Modules:
  0.0 469.3 jit_solution(7924358330212764768)
XLA Ops:
  6.5 0.0 copy-start
  6.5 0.0 all-gather.2.cloned.1.call-start
  6.5 0.7 all-gather.2.cloned.1.call-update
  7.3 0.0 reduce-scatter.2.cloned.1.call-start
  8.0 0.7 compare_select_fusion
  8.7 0.7 compare_select_fusion.1
  9.3 58.8 %all-gather.2.cloned.1.call-done = bf16[32768,128]{1,0:T(8,128)(2,1)} async-done(((bf16[2048,128]{1,0:T(8,128)(2,1)}), bf16[32768,128]{1,0:T(8,128)(2,1)}) %all-gather.2.cloned.1.call-update) | async-done | bytes 8388624 | tf_op jit(solution)/shard_map/all_gather | solution.py:17
  68.1 12.0 %gather_fusion = bf16[256,128,128]{2,1,0:T(8,128)(2,1)} fusion(bf16[256,128,128]{2,1,0:T(8,128)(2,1)} %bitcast.18, s32[1024]{0:T(1024)S(1)} %pad_clamp_fusion), kind=kCustom, calls=%fused_computation | custom fusion | bytes 16778240 | tf_op jit(solution)/shard_map/gather | solution.py:23
  80.1 13.2 %select_bitcast_fusion = f32[256,128,128]{1,2,0:T(8,128)} fusion(bf16[256,128,128]{2,1,0:T(8,128)(2,1)} %gather_fusion, bf16[1,1,256,128,128]{4,3,2,1,0:T(8,128)(2,1)} %param.8, pred[256]{0:T(512)(128)(4,1)S(1)} %iota_compare_fusion), kind=kOutput, calls=%fused_computation.2 | convolution fusion | flops 1077936128 | bytes 33554688 | tf_op jit(solution)/shard_map/kij,kjf->kif/dot_general | solution.py:22
  93.3 17.4 %copy.10 = f32[256,128,128]{2,1,0:T(8,128)} copy(f32[256,128,128]{1,2,0:T(8,128)} %select_bitcast_fusion) | data formatting | bytes 33554432 | tf_op jit(solution)/shard_map/jit(_where)/select_n | solution.py:25
  110.7 7.8 %broadcast_in_dim.12 = f32[256,128,128]{2,1,0:T(8,128)} broadcast(f32[]{:T(128)} %constant.3.clone.1), dimensions={} | broadcast | bytes 16777220 | tf_op jit(solution)/shard_map/broadcast_in_dim | solution.py:20
  118.6 54.2 %scatter_fusion = f32[256,128,128]{2,1,0:T(8,128)} fusion(f32[256,128,128]{2,1,0:T(8,128)} %broadcast_in_dim.12, s32[256]{0:T(256)S(1)} %bitcast.19, f32[256,128,128]{2,1,0:T(8,128)} %copy.10), kind=kCustom, calls=%fused_computation.1 | custom fusion | flops 4194304 | bytes 50332672 | tf_op jit(solution)/shard_map/scatter-add | solution.py:26
  172.8 0.0 copy-start.1
  172.8 0.0 reduce-scatter.2.cloned.1.call-update
  172.8 287.1 %reduce-scatter.2.cloned.1.call-done = f32[2048,128]{1,0:T(8,128)} async-done(((f32[32768,128]{1,0:T(8,128)}), f32[2048,128]{1,0:T(8,128)}) %reduce-scatter.2.cloned.1.call-update) | async-done | bytes 1048592 | tf_op jit(solution)/shard_map/reduce_scatter | solution.py:27
  459.9 0.0 copy-done
  459.9 0.0 copy-done.1
  459.9 2.6 fusion.2
  (2 shorter events, 0.0 us)
Async XLA Ops:
  6.5 453.4 %copy-start = (bf16[128,256]{1,0:T(8,128)(2,1)S(1)}, bf16[128,256]{1,0:T(8,128)(2,1)}, u32[]{:S(2)}) copy-start(bf16[128,256]{1,0:T(8,128)(2,1)} %param.12) | copy-start | bytes 196612
  6.5 61.6 %all-gather.2.cloned.1.call-start = ((), (), s32[]{:S(2)}) async-start(), calls=%async_computation.1 | async-start | bytes 8912896 | tf_op jit(solution)/shard_map/all_gather | solution.py:17
  7.3 452.6 %reduce-scatter.2.cloned.1.call-start = ((), (), s32[]{:S(2)}) async-start(), calls=%async_computation.2 | async-start | bytes 17825792 | tf_op jit(solution)/shard_map/reduce_scatter | solution.py:27
  172.8 287.1 %copy-start.1 = (f32[256]{0:T(256)S(1)}, f32[256]{0:T(256)}, u32[]{:S(2)}) copy-start(f32[256]{0:T(256)} %param.13) | copy-start | bytes 3076
Sparse Core Ops, SparseCore 0:
  9.2 58.8 all-gather.1
  172.9 286.9 reduce-scatter.1
where the time goes:
time: 470 us; the launch traced here: 469 us
  waiting for transfers between devices  347 us (74%)
  other arithmetic  55.6 us (12%)
  local copies, waits for them, and re-layouts  37.3 us (8%)
  matrix products  15.8 us (3%)
  between operations  14.1 us (3%)
    reduce_scatter x1, waiting for transfers between devices, on_device(): lax.psum_scatter(partial_value.reshape(-1, feat_width), 'col', scatter_di...  287 us
    all_gather x1, waiting for transfers between devices, on_device(): gathered = lax.all_gather(node_feats, 'row', axis=0, tiled=True)  58.8 us
    scatter-add x1, other arithmetic, on_device(): partial_value = partial_value.at[dest_ids].add(products)  54.2 us
    select_n x1, local copies, waits for them, and re-layouts, on_device(): products = jnp.where(is_live[:, None, None], products, 0.0)  17.4 us
    dot_general x1, matrix products, on_device(): jnp.einsum('kij,kjf->kif', tile_set, blocks[source_ids], preferred_elemen...  13.2 us
    gather x1, local copies, waits for them, and re-layouts, on_device(): blocks[source_ids]  12 us
  transfers between devices with their start and end apart: 2, of which 2 were waited for; matrix products, arithmetic and copies ran while one was open for 0% of the time, Pallas kernels for 0%

commit v1 on v0

v1 whole, which is shorter than its diff:
```python
import functools

import jax
import jax.numpy as jnp
from jax import lax
from jax.experimental import pallas as pl
from jax.experimental.pallas import tpu as pltpu
from jax.sharding import PartitionSpec as P

TILE = 128
TPD = 16
SLOTS = 256
NY, NXLO, NCORE = 4, 2, 2
NZ, NXHI = 8, 2
ROWS = TPD * TILE
HALF_SLOTS = 8
OWN_BLOCKS = NZ * TPD
OTHER_BLOCKS = NZ * HALF_SLOTS
TRASH = OWN_BLOCKS
GROUP = 8
LIST = SLOTS + GROUP
MAP_AT = 2 * LIST
COUNT_AT = MAP_AT + OTHER_BLOCKS
PLAN = 640
THIRDS = (688, 688, 672)
LOAD = 32

VMEM = pltpu.VMEM
SMEM_SPEC = pl.BlockSpec(memory_space=pltpu.SMEM)
VMEM_SPEC = pl.BlockSpec(memory_space=pltpu.VMEM)
ANY_SPEC = pl.BlockSpec(memory_space=pl.ANY)


def row_perm(change):
    pairs = []
    for y in range(NY):
        for x in range(NXLO):
            for k in range(NCORE):
                ty, tx, tk = change(y, x, k)
                pairs.append(((y * NXLO + x) * NCORE + k, (ty % NY * NXLO + tx) * NCORE + tk))
    return pairs


FROM_UP = row_perm(lambda y, x, k: (y - 1, x, k))
FROM_DOWN = row_perm(lambda y, x, k: (y + 1, x, k))
FROM_SIDE = row_perm(lambda y, x, k: (y, 1 - x, k))
FROM_CORE = row_perm(lambda y, x, k: (y, x, 1 - k))
Z_PLUS = [(z * NXHI + x, (z + 1) % NZ * NXHI + x) for z in range(NZ) for x in range(NXHI)]
Z_MINUS = [(z * NXHI + x, (z - 1) % NZ * NXHI + x) for z in range(NZ) for x in range(NXHI)]
X_FLIP = [(z * NXHI + x, z * NXHI + 1 - x) for z in range(NZ) for x in range(NXHI)]


def plan_kernel(place, dest, source, partner_dest, plan, slot_of, used):
    my_y, my_x, my_k, my_z, my_xhi = (place[i] for i in range(5))

    def clear(i, _):
        slot_of[i] = -1
        return 0

    def clear_lists(i, _):
        plan[i] = TRASH << 16
        return 0

    lax.fori_loop(0, SLOTS, clear, 0, unroll=8)
    lax.fori_loop(0, MAP_AT, clear_lists, 0, unroll=8)

    def clear_map(i, _):
        plan[MAP_AT + i] = TPD
        return 0

    lax.fori_loop(0, OTHER_BLOCKS, clear_map, 0, unroll=8)
    for i in range(2 * NZ):
        used[i] = 0

    def slot_for(block, away, at):
        held = slot_of[block]
        is_new = held < 0
        count = used[at + away]
        slot = jnp.where(is_new, count, held)
        slot_of[block] = slot
        used[at + away] = count + is_new.astype(jnp.int32)
        return slot

    def split(block):
        col = block // TPD
        away = (col // NXHI - my_z + NZ) % NZ
        return away, col % NXHI, block % TPD

    def place_tile(i, carry):
        block = dest[i]
        s = source[i]
        row = s // TPD
        rel_y = (row // (NXLO * NCORE) - my_y + NY) % NY
        rel_x = (row // NCORE % NXLO - my_x + NXLO) % NXLO
        rel_k = (row % NCORE - my_k + NCORE) % NCORE
        rel = ((rel_y * NXLO + rel_x) * NCORE + rel_k) * TPD + s % TPD
        away, half, inner = split(jnp.maximum(block, 0))

        def other(c):
            slot = slot_for(block, away, 0)
            plan[c[0]] = i | (rel << 8) | ((away * HALF_SLOTS + slot) << 16)
            return c[0] + 1, c[1]

        def own(c):
            plan[LIST + c[1]] = i | (rel << 8) | ((away * TPD + inner) << 16)
            return c[0], c[1] + 1

        def live(c):
            return lax.cond(half == my_xhi, own, other, c)

        return lax.cond(block >= 0, live, lambda c: c, carry)

    n_other, n_own = lax.fori_loop(0, SLOTS, place_tile, (jnp.int32(0), jnp.int32(0)))

    def place_partner(i, _):
        block = partner_dest[i]
        away, half, inner = split(jnp.maximum(block, 0))

        @pl.when((block >= 0) & (half == my_xhi))
        def _():
            slot = slot_for(block, away, NZ)
            plan[MAP_AT + away * HALF_SLOTS + slot] = inner

        return 0

    lax.fori_loop(0, SLOTS, place_partner, 0)
    plan[COUNT_AT] = (n_other + GROUP - 1) // GROUP
    plan[COUNT_AT + 1] = (n_own + GROUP - 1) // GROUP
    plan[COUNT_AT + 2] = n_other + n_own


def make_plan(place, dest, source, partner_dest):
    return pl.pallas_call(
        plan_kernel,
        out_shape=jax.ShapeDtypeStruct((PLAN,), jnp.int32),
        in_specs=[SMEM_SPEC] * 4,
        out_specs=SMEM_SPEC,
        scratch_shapes=[pltpu.SMEM((SLOTS,), jnp.int32), pltpu.SMEM((2 * NZ,), jnp.int32)],
        name="plan",
    )(place, dest, source, partner_dest)


def add_products(plan, first, groups, tiles, feats, acc):
    def one_group(g, _):
        entries = [plan[first + g * GROUP + i] for i in range(GROUP)]
        products = [
            jnp.dot(
                tiles[e & 255],
                feats[pl.ds(pl.multiple_of(((e >> 8) & 255) * TILE, TILE), TILE), :],
                preferred_element_type=jnp.float32,
            )
            for e in entries
        ]
        for e, product in zip(entries, products):
            acc[e >> 16] += product
        return 0

    lax.fori_loop(0, groups, one_group, 0)


def other_kernel(pieces, plan, *refs):
    tiles_hbm = refs[0]
    feats_hbm = refs[1 : 1 + len(pieces)]
    refs = refs[1 + len(pieces) :]
    sends, (tiles, feats, acc, sems) = refs[:NZ], refs[NZ:]
    feat_copies = [
        pltpu.make_async_copy(src, feats.at[pl.ds(at, n), :], sems.at[0])
        for src, (at, n) in zip(feats_hbm, pieces)
    ]
    for copy in feat_copies:
        copy.start()

    def tile_copy(j):
        at = pl.ds(j * LOAD, LOAD)
        return pltpu.make_async_copy(tiles_hbm.at[at], tiles.at[at], sems.at[1])

    for j in range(SLOTS // LOAD):
        tile_copy(j).start()

    def clear(i, _):
        acc[i] = jnp.zeros((TILE, acc.shape[2]), jnp.float32)
        return 0

    lax.fori_loop(0, OTHER_BLOCKS, clear, 0, unroll=4)
    for j in range(SLOTS // LOAD):
        tile_copy(j).wait()
    for copy in feat_copies:
        copy.wait()
    add_products(plan, 0, plan[COUNT_AT], tiles, feats, acc)
    for away, send in enumerate(sends):
        send[...] = acc[pl.ds(away * HALF_SLOTS, HALF_SLOTS)].astype(send.dtype)


def own_kernel(plan, tiles, feats, *refs):
    chunks, acc = refs[:NZ], refs[NZ]

    def clear(i, _):
        acc[i] = jnp.zeros((TILE, acc.shape[2]), jnp.float32)
        return 0

    lax.fori_loop(0, OWN_BLOCKS, clear, 0, unroll=4)
    add_products(plan, LIST, plan[COUNT_AT + 1], tiles, feats, acc)
    for away, chunk in enumerate(chunks):
        chunk[...] = acc[pl.ds(away * TPD, TPD)]


def gather_compute(plan, tile_set, pieces, arrays, width):
    bf = jnp.bfloat16
    block = lambda n, dtype: jax.ShapeDtypeStruct((n, TILE, width), dtype)
    outs = pl.pallas_call(
        functools.partial(other_kernel, pieces),
        out_shape=[block(HALF_SLOTS, bf)] * NZ
        + [VMEM((SLOTS, TILE, TILE), bf), VMEM((SLOTS * TILE, width), bf)],
        in_specs=[SMEM_SPEC] + [ANY_SPEC] * (1 + len(arrays)),
        out_specs=[VMEM_SPEC] * (NZ + 2),
        scratch_shapes=[
            VMEM((TRASH + 1, TILE, width), jnp.float32),
            pltpu.SemaphoreType.DMA((2,)),
        ],
        compiler_params=pltpu.CompilerParams(vmem_limit_bytes=40 << 20),
        name="other_half",
    )(plan, tile_set, *arrays)
    sends, tiles, feats = outs[:NZ], outs[NZ], outs[NZ + 1]
    tiles = pltpu.with_memory_space_constraint(tiles, pltpu.VMEM)
    feats = pltpu.with_memory_space_constraint(feats, pltpu.VMEM)

    def own_part():
        return pl.pallas_call(
            own_kernel,
            out_shape=[block(TPD, jnp.float32)] * NZ,
            in_specs=[SMEM_SPEC, VMEM_SPEC, VMEM_SPEC],
            out_specs=[VMEM_SPEC] * NZ,
            scratch_shapes=[VMEM((TRASH + 1, TILE, width), jnp.float32)],
            compiler_params=pltpu.CompilerParams(vmem_limit_bytes=40 << 20),
            name="own_half",
        )(plan, tiles, feats)

    return sends, own_part


def merge(away, plan, own, arrived, passed, acc):
    acc[pl.ds(0, TPD)] = own[...]
    for ref, at in passed:
        n = ref.shape[0]
        acc[pl.ds(at, n)] += ref[...].astype(jnp.float32)
    for i in range(HALF_SLOTS):
        acc[plan[MAP_AT + away * HALF_SLOTS + i]] += arrived[i].astype(jnp.float32)


def hop_kernel(away, pass_at, cuts, plan, own, arrived, *refs):
    passed = list(zip(refs[: len(pass_at)], pass_at))
    outs, acc = refs[len(pass_at) : -1], refs[-1]
    merge(away, plan, own, arrived, passed, acc)
    for out, (at, n) in zip(outs, cuts):
        out[...] = acc[pl.ds(at, n)].astype(out.dtype)


def hop(away, plan, own, arrived, passed, pass_at, cuts):
    width = own.shape[-1]
    out = pl.pallas_call(
        functools.partial(hop_kernel, away, pass_at, cuts),
        out_shape=[jax.ShapeDtypeStruct((n, TILE, width), jnp.bfloat16) for _, n in cuts],
        in_specs=[SMEM_SPEC] + [VMEM_SPEC] * (2 + len(passed)),
        out_specs=[VMEM_SPEC] * len(cuts),
        scratch_shapes=[VMEM((TPD + 1, TILE, width), jnp.float32)],
        name=f"hop_{away}",
    )(plan, own, arrived, *passed)
    return out


def last_kernel(plan, own, arrived, passed_a, passed_b, weight, bias, out, acc):
    merge(0, plan, own, arrived, [(passed_a, 0), (passed_b, 0)], acc)
    total = acc[pl.ds(0, TPD)].reshape(ROWS, -1).astype(jnp.bfloat16)
    hidden = jnp.dot(total, weight[...], preferred_element_type=jnp.float32) + bias[...]
    out[...] = jnp.maximum(hidden, 0.0).astype(out.dtype)


def last(plan, own, arrived, passed_a, passed_b, weight, bias):
    return pl.pallas_call(
        last_kernel,
        out_shape=jax.ShapeDtypeStruct((ROWS, weight.shape[1]), jnp.bfloat16),
        in_specs=[SMEM_SPEC] + [VMEM_SPEC] * 6,
        out_specs=VMEM_SPEC,
        scratch_shapes=[VMEM((TPD + 1, TILE, own.shape[-1]), jnp.float32)],
        name="last",
    )(plan, own, arrived, passed_a, passed_b, weight, bias)


def gather(mine):
    send = lambda array, perm: lax.ppermute(array, "row", perm)
    got = [(0, 0, 0, ROWS, mine)]
    up, down, side = send(mine, FROM_UP), send(mine, FROM_DOWN), send(mine, FROM_SIDE)
    got += [(1, 0, 0, ROWS, up), (3, 0, 0, ROWS, down), (0, 1, 0, ROWS, side)]
    far = send(up, FROM_UP)
    down_side = send(side, FROM_DOWN)
    up_side = send(up, FROM_SIDE)
    got += [(2, 0, 0, ROWS, far), (3, 1, 0, ROWS, down_side), (1, 1, 0, ROWS, up_side)]
    at = 0
    for n, array, perm in zip(
        THIRDS, (up_side, down_side, far), (FROM_UP, FROM_DOWN, FROM_SIDE)
    ):
        got.append((2, 1, at, n, send(array[at : at + n], perm)))
        at += n
    pieces, arrays = [], []
    for y, x, first, n, array in got:
        for k in range(NCORE):
            pieces.append((((y * NXLO + x) * NCORE + k) * ROWS + first, n))
            arrays.append(array if k == 0 else send(array, FROM_CORE))
    return tuple(pieces), arrays


def on_device(node_feats, tile_vals, tile_dest, tile_source, tile_count, weight, out_bias):
    row, col = lax.axis_index("row"), lax.axis_index("col")
    place = jnp.stack(
        [row // (NXLO * NCORE), row // NCORE % NXLO, row % NCORE, col // NXHI, col % NXHI]
    ).astype(jnp.int32)
    slots = jnp.arange(SLOTS, dtype=jnp.int32)
    dest = jnp.where(slots < tile_count[0, 0], tile_dest[0, 0], -1)
    partner_dest = lax.ppermute(dest, "col", X_FLIP)
    pieces, arrays = gather(node_feats)
    plan = make_plan(place, dest, tile_source[0, 0], partner_dest)
    sends, own_part = gather_compute(plan, tile_vals[0, 0], pieces, arrays, node_feats.shape[1])
    order = (4, 3, 5, 2, 6, 1, 7, 0)
    arrived = {}
    for away in order:
        arrived[away] = lax.ppermute(sends[away], "col", X_FLIP)
    own = own_part()
    half = TPD // 2
    plus, minus = hop(
        4, plan, own[4], arrived[4], (), (), ((0, half), (half, half))
    )
    plus, minus = lax.ppermute(plus, "col", Z_PLUS), lax.ppermute(minus, "col", Z_MINUS)
    for step, (a, b) in enumerate(((3, 5), (2, 6), (1, 7))):
        at_a, at_b = ((0,), (half,)) if step == 0 else ((0,), (0,))
        (plus,) = hop(a, plan, own[a], arrived[a], (plus,), at_a, ((0, TPD),))
        plus = lax.ppermute(plus, "col", Z_PLUS)
        (minus,) = hop(b, plan, own[b], arrived[b], (minus,), at_b, ((0, TPD),))
        minus = lax.ppermute(minus, "col", Z_MINUS)
    return last(plan, own[0], arrived[0], plus, minus, weight, out_bias.reshape(1, -1))


def solution(mesh):
    return jax.shard_map(
        on_device,
        mesh=mesh,
        in_specs=(
            P(("row", "col"), None),
            P("row", "col", None, None, None),
            P("row", "col", None),
            P("row", "col", None),
            P("row", "col"),
            P(),
            P(),
        ),
        out_specs=P(("row", "col"), None),
        check_vma=False,
    )
```

time: 470 us -> 181 us (0.39)
  the two profiles are of different devices: /device:TPU:1 before, /device:TPU:2 now
where the time goes in v1:
time: 181 us; the launch traced here: 180 us
  waiting for transfers between devices  62.2 us (34%)
  Pallas kernels  61.3 us (34%)
  starting transfers between devices  46.9 us (26%)
  local copies, waits for them, and re-layouts  8.26 us (5%)
    ppermute x19, waiting for transfers between devices, gather(): send = lambda array, perm: lax.ppermute(array, 'row', perm)  27.8 us
    pallas_call x1, Pallas kernels, make_plan(): pl.pallas_call(plan_kernel, out_shape=jax.ShapeDtypeStruct((PLAN,), jnp.i...  25.2 us
    ppermute x8, waiting for transfers between devices, on_device(): arrived[away] = lax.ppermute(sends[away], 'col', X_FLIP)  21.9 us
    pallas_call x7, Pallas kernels, hop(): pl.pallas_call(functools.partial(hop_kernel, away, pass_at, cuts), out_sh...  16.9 us
    ppermute x19, starting transfers between devices, gather(): send = lambda array, perm: lax.ppermute(array, 'row', perm)  16 us
    ppermute x8, starting transfers between devices, on_device(): arrived[away] = lax.ppermute(sends[away], 'col', X_FLIP)  14.4 us
    ppermute x3, starting transfers between devices, on_device(): minus = lax.ppermute(minus, 'col', Z_MINUS)  9.81 us
    pallas_call x1, Pallas kernels, gather_compute(): pl.pallas_call(functools.partial(other_kernel, pieces), out_shape=[block(...  9.57 us
  transfers between devices with their start and end apart: 36, of which 11 were waited for; matrix products, arithmetic and copies ran while one was open for 1% of the time, Pallas kernels for 27%

profile of v1, /device:TPU:2, one launch (start us, length us, event | category | flops | bytes accessed | tf_op | source)
XLA Modules:
  0.0 180.4 jit_solution(10277994565008895960)
XLA Ops:
  0.0 3.0 %collective-permute-start.2 = (bf16[2048,128]{1,0:T(8,128)(2,1)}, bf16[2048,128]{1,0:T(8,128)(2,1)S(1)}, u32[]{:S(2)}, u32[]{:S(2)}) collective-permute-start(bf16[2048,128]{1,0:T(8,128)(2,1)} %refs_1_.1), channel_id=1, source_target_pairs={{0,192},{16,208},{32,224},{48,240},{64,0},{80,16},{96,32},{112,48}... | collective-permute-start | bytes 1572872 | tf_op jit(solution)/shard_map/ppermute | solution.py:290
  3.0 1.3 collective-permute-start.6
  4.3 10.2 %collective-permute-done.2.refs_3_ = bf16[2048,128]{1,0:T(8,128)(2,1)S(1)} collective-permute-done((bf16[2048,128]{1,0:T(8,128)(2,1)}, bf16[2048,128]{1,0:T(8,128)(2,1)S(1)}, u32[]{:S(2)}, u32[]{:S(2)}) %collective-permute-start.2) | collective-permute-done | bytes 524320 | tf_op jit(solution)/shard_map/ppermute | solution.py:290
  14.5 0.5 collective-permute-start.12
  15.1 3.6 %collective-permute-start.8 = (bf16[2048,128]{1,0:T(8,128)(2,1)S(1)}, bf16[2048,128]{1,0:T(8,128)(2,1)S(1)}, u32[]{:S(2)}, u32[]{:S(2)}) collective-permute-start(bf16[2048,128]{1,0:T(8,128)(2,1)S(1)} %collective-permute-done.2.refs_3_), channel_id=1, source_target_pairs={{0,192},{16,208},{32,224},{48,240},{64,0},{80,16},{96,32},{112,48}... | collective-permute-start | bytes 1572872 | tf_op jit(solution)/shard_map/ppermute | solution.py:290
  19.3 0.7 compare_select_fusion.dest
  20.0 2.4 %collective-permute-start = (s32[256]{0:T(256)S(1)}, s32[256]{0:T(256)S(1)}, u32[]{:S(2)}, u32[]{:S(2)}) collective-permute-start(s32[256]{0:T(256)S(1)} %compare_select_fusion.dest), channel_id=1, source_target_pairs={{0,1},{1,0},{2,3},{3,2},{4,5},{5,4},{6,7},{7,6},{8,9},{9,8},{10,11... | collective-permute-start | bytes 3080 | tf_op jit(solution)/shard_map/ppermute | solution.py:319
  22.4 6.4 %collective-permute-done.partner_dest = s32[256]{0:T(256)S(1)} collective-permute-done((s32[256]{0:T(256)S(1)}, s32[256]{0:T(256)S(1)}, u32[]{:S(2)}, u32[]{:S(2)}) %collective-permute-start) | collective-permute-done | bytes 1056 | tf_op jit(solution)/shard_map/ppermute | solution.py:319
  28.8 0.5 collective-permute-start.5
  29.3 0.1 collective-permute-start.3
  29.4 0.4 collective-permute-start.10
  29.8 0.1 collective-permute-start.7
  30.0 0.9 collective-permute-done.1.refs_2_
  30.9 1.8 collective-permute-start.18
  32.7 3.0 %collective-permute-start.14 = (bf16[688,128]{1,0:T(8,128)(2,1)S(1)}, bf16[688,128]{1,0:T(8,128)(2,1)S(1)}, u32[]{:S(2)}, u32[]{:S(2)}) collective-permute-start(bf16[688,128]{1,0:T(8,128)(2,1)S(1)} %slice.12), channel_id=1, source_target_pairs={{0,192},{16,208},{32,224},{48,240},{64,0},{80,16},{96,32},{112,48}... | collective-permute-start | bytes 528392 | tf_op jit(solution)/shard_map/ppermute | solution.py:290
  35.8 9.2 %collective-permute-done.10.refs_11_ = bf16[2048,128]{1,0:T(8,128)(2,1)S(1)} collective-permute-done((bf16[2048,128]{1,0:T(8,128)(2,1)S(1)}, bf16[2048,128]{1,0:T(8,128)(2,1)S(1)}, u32[]{:S(2)}, u32[]{:S(2)}) %collective-permute-start.10) | collective-permute-done | bytes 524320 | tf_op jit(solution)/shard_map/ppermute | solution.py:290
  45.0 0.6 collective-permute-start.11
  45.6 0.2 copy-done.9
  45.8 0.6 collective-permute-start.19
  46.4 7.5 %collective-permute-done.16.refs_17_ = bf16[688,128]{1,0:T(8,128)(2,1)S(1)} collective-permute-done((bf16[688,128]{1,0:T(8,128)(2,1)S(1)}, bf16[688,128]{1,0:T(8,128)(2,1)S(1)}, u32[]{:S(2)}, u32[]{:S(2)}) %collective-permute-start.16) | collective-permute-done | bytes 176160 | tf_op jit(solution)/shard_map/ppermute | solution.py:290
  53.9 0.7 copy-done.29
  54.6 0.5 collective-permute-start.17
  55.1 0.7 stack.23.place
  55.7 25.2 %plan.1 = s32[640]{0:T(1024)} custom-call(s32[5]{0:T(128)} %stack.23.place, s32[256]{0:T(256)} %copy-done.30, s32[256]{0:T(256)} %bitcast.13, s32[256]{0:T(256)} %copy-done.31), custom_call_target="tpu_custom_call" | custom-call | tf_op jit(solution)/shard_map/plan/pallas_call | solution.py:133
  81.0 9.6 %other_half.1 = (bf16[8,128,128]{2,1,0:T(8,128)(2,1)}, bf16[8,128,128]{2,1,0:T(8,128)(2,1)}, bf16[8,128,128]{2,1,0:T(8,128)(2,1)}, bf16[8,128,128]{2,1,0:T(8,128...) custom-call(s32[640]{0:T(1024)} %plan.1, ...), custom_call_target="tpu_custom_call" | custom-call | tf_op jit(solution)/shard_map/other_half/pallas_call | solution.py:210
  90.6 2.4 %collective-permute-start.24 = (bf16[8,128,128]{2,1,0:T(8,128)(2,1)}, bf16[8,128,128]{2,1,0:T(8,128)(2,1)S(1)}, u32[]{:S(2)}, u32[]{:S(2)}) collective-permute-start(bf16[8,128,128]{2,1,0:T(8,128)(2,1)} %get-tuple-element.36), channel_id=1, source_target_pairs={{0,1},{1,0},{2,3},{3,2},{4,5},{5,4},{6,7},{7,6},{8,9},{9,8},{10,11... | collective-permute-start | bytes 786440 | tf_op jit(solution)/shard_map/ppermute | solution.py:326
  93.0 1.3 collective-permute-start.31
  94.2 6.4 %own_half.1 = (f32[16,128,128]{2,1,0:T(8,128)}, f32[16,128,128]{2,1,0:T(8,128)}, f32[16,128,128]{2,1,0:T(8,128)}, f32[16,128,128]{2,1,0:T(8,128)}, f32[16,128,12...) custom-call(s32[640]{0:T(1024)} %plan.1, ...), custom_call_target="tpu_custom_call" | custom-call | tf_op jit(solution)/shard_map/own_half/pallas_call | solution.py:228
  100.7 0.7 collective-permute-done.24.arrived
  101.3 0.7 copy-done.18
  102.1 2.2 %hop_4.1 = (bf16[8,128,128]{2,1,0:T(8,128)(2,1)}, bf16[8,128,128]{2,1,0:T(8,128)(2,1)}) custom-call(s32[640]{0:T(1024)} %plan.1, f32[16,128,128]{2,1,0:T(8,128)} %get-tuple-element.35.own, bf16[8,128,128]{2,1,0:T(8,128)(2,1)} %copy-done.18), custom_call_target="tpu_custom_call" | custom-call | tf_op jit(solution)/shard_map/hop_4/pallas_call | solution.py:260
  104.3 4.3 %collective-permute-start.32 = (bf16[8,128,128]{2,1,0:T(8,128)(2,1)}, bf16[8,128,128]{2,1,0:T(8,128)(2,1)S(1)}, u32[]{:S(2)}, u32[]{:S(2)}) collective-permute-start(bf16[8,128,128]{2,1,0:T(8,128)(2,1)} %get-tuple-element.44), channel_id=1, source_target_pairs={{0,14},{1,15},{2,0},{3,1},{4,2},{5,3},{6,4},{7,5},{8,6},{9,7},{10,... | collective-permute-start | bytes 786440 | tf_op jit(solution)/shard_map/ppermute | solution.py:332
  108.6 3.2 %collective-permute-start.23 = (bf16[8,128,128]{2,1,0:T(8,128)(2,1)S(1)}, bf16[8,128,128]{2,1,0:T(8,128)(2,1)S(1)}, u32[]{:S(2)}, u32[]{:S(2)}) collective-permute-start(bf16[8,128,128]{2,1,0:T(8,128)(2,1)S(1)} %copy-done.37), channel_id=1, source_target_pairs={{0,1},{1,0},{2,3},{3,2},{4,5},{5,4},{6,7},{7,6},{8,9},{9,8},{10,11... | collective-permute-start | bytes 786440 | tf_op jit(solution)/shard_map/ppermute | solution.py:326
  111.8 3.4 %collective-permute-done.32.refs_0_ = bf16[8,128,128]{2,1,0:T(8,128)(2,1)S(1)} collective-permute-done((bf16[8,128,128]{2,1,0:T(8,128)(2,1)}, bf16[8,128,128]{2,1,0:T(8,128)(2,1)S(1)}, u32[]{:S(2)}, u32[]{:S(2)}) %collective-permute-start.32) | collective-permute-done | bytes 262176 | tf_op jit(solution)/shard_map/ppermute | solution.py:332
  115.2 0.7 copy-done.25
  115.9 2.3 %hop_5.1 = bf16[16,128,128]{2,1,0:T(8,128)(2,1)} custom-call(s32[640]{0:T(1024)} %plan.1, f32[16,128,128]{2,1,0:T(8,128)} %get-tuple-element.42.own, bf16[8,128,128]{2,1,0:T(8,128)(2,1)} %copy-done.22, bf16[8,128,128]{2,1,0:T(8,128)(2,1)} %copy-done.25), custom_call_target="tpu_custom_call" | custom-call | tf_op jit(solution)/shard_map/hop_5/pallas_call | solution.py:260
  118.3 3.6 %collective-permute-start.33 = (bf16[16,128,128]{2,1,0:T(8,128)(2,1)}, bf16[16,128,128]{2,1,0:T(8,128)(2,1)S(1)}, u32[]{:S(2)}, u32[]{:S(2)}) collective-permute-start(bf16[16,128,128]{2,1,0:T(8,128)(2,1)} %hop_5.1), channel_id=1, source_target_pairs={{0,14},{1,15},{2,0},{3,1},{4,2},{5,3},{6,4},{7,5},{8,6},{9,7},{10,... | collective-permute-start | bytes 1572872 | tf_op jit(solution)/shard_map/ppermute | solution.py:338
  121.9 0.7 copy-done.23
  122.6 2.3 %hop_3.1 = bf16[16,128,128]{2,1,0:T(8,128)(2,1)} custom-call(s32[640]{0:T(1024)} %plan.1, f32[16,128,128]{2,1,0:T(8,128)} %get-tuple-element.33.own, bf16[8,128,128]{2,1,0:T(8,128)(2,1)} %copy-done.23, bf16[8,128,128]{2,1,0:T(8,128)(2,1)} %copy-done.24), custom_call_target="tpu_custom_call" | custom-call | tf_op jit(solution)/shard_map/hop_3/pallas_call | solution.py:260
  125.0 0.8 collective-permute-start.30
  125.8 2.7 %collective-permute-start.22 = (bf16[8,128,128]{2,1,0:T(8,128)(2,1)S(1)}, bf16[8,128,128]{2,1,0:T(8,128)(2,1)S(1)}, u32[]{:S(2)}, u32[]{:S(2)}) collective-permute-start(bf16[8,128,128]{2,1,0:T(8,128)(2,1)S(1)} %copy-done.35), channel_id=1, source_target_pairs={{0,1},{1,0},{2,3},{3,2},{4,5},{5,4},{6,7},{7,6},{8,9},{9,8},{10,11... | collective-permute-start | bytes 786440 | tf_op jit(solution)/shard_map/ppermute | solution.py:326
  128.5 7.1 %collective-permute-done.30.arrived = bf16[8,128,128]{2,1,0:T(8,128)(2,1)S(1)} collective-permute-done((bf16[8,128,128]{2,1,0:T(8,128)(2,1)S(1)}, bf16[8,128,128]{2,1,0:T(8,128)(2,1)S(1)}, u32[]{:S(2)}, u32[]{:S(2)}) %collective-permute-start.30) | collective-permute-done | bytes 262176 | tf_op jit(solution)/shard_map/ppermute | solution.py:326
  135.7 0.7 copy-done.20
  136.4 0.2 copy-done.12
  136.6 2.5 %hop_6.1 = bf16[16,128,128]{2,1,0:T(8,128)(2,1)} custom-call(s32[640]{0:T(1024)} %plan.1, f32[16,128,128]{2,1,0:T(8,128)} %get-tuple-element.40.own, bf16[8,128,128]{2,1,0:T(8,128)(2,1)} %copy-done.20, bf16[16,128,128]{2,1,0:T(8,128)(2,1)} %copy-done.12), custom_call_target="tpu_custom_call" | custom-call | tf_op jit(solution)/shard_map/hop_6/pallas_call | solution.py:260
  139.1 3.3 %collective-permute-start.34 = (bf16[16,128,128]{2,1,0:T(8,128)(2,1)}, bf16[16,128,128]{2,1,0:T(8,128)(2,1)S(1)}, u32[]{:S(2)}, u32[]{:S(2)}) collective-permute-start(bf16[16,128,128]{2,1,0:T(8,128)(2,1)} %hop_6.1), channel_id=1, source_target_pairs={{0,14},{1,15},{2,0},{3,1},{4,2},{5,3},{6,4},{7,5},{8,6},{9,7},{10,... | collective-permute-start | bytes 1572872 | tf_op jit(solution)/shard_map/ppermute | solution.py:338
  142.4 0.7 copy-done.16
  143.1 0.2 copy-done.13
  143.3 2.5 %hop_2.1 = bf16[16,128,128]{2,1,0:T(8,128)(2,1)} custom-call(s32[640]{0:T(1024)} %plan.1, f32[16,128,128]{2,1,0:T(8,128)} %get-tuple-element.31.own, bf16[8,128,128]{2,1,0:T(8,128)(2,1)} %copy-done.16, bf16[16,128,128]{2,1,0:T(8,128)(2,1)} %copy-done.13), custom_call_target="tpu_custom_call" | custom-call | tf_op jit(solution)/shard_map/hop_2/pallas_call | solution.py:260
  145.7 0.9 collective-permute-start.29
  146.6 2.6 %collective-permute-start.21 = (bf16[8,128,128]{2,1,0:T(8,128)(2,1)S(1)}, bf16[8,128,128]{2,1,0:T(8,128)(2,1)S(1)}, u32[]{:S(2)}, u32[]{:S(2)}) collective-permute-start(bf16[8,128,128]{2,1,0:T(8,128)(2,1)S(1)} %copy-done.33), channel_id=1, source_target_pairs={{0,1},{1,0},{2,3},{3,2},{4,5},{5,4},{6,7},{7,6},{8,9},{9,8},{10,11... | collective-permute-start | bytes 786440 | tf_op jit(solution)/shard_map/ppermute | solution.py:326
  149.3 6.7 %collective-permute-done.29.arrived = bf16[8,128,128]{2,1,0:T(8,128)(2,1)S(1)} collective-permute-done((bf16[8,128,128]{2,1,0:T(8,128)(2,1)S(1)}, bf16[8,128,128]{2,1,0:T(8,128)(2,1)S(1)}, u32[]{:S(2)}, u32[]{:S(2)}) %collective-permute-start.29) | collective-permute-done | bytes 262176 | tf_op jit(solution)/shard_map/ppermute | solution.py:326
  156.0 0.7 copy-done.21
  156.7 0.2 copy-done.14
  156.9 2.5 %hop_7.1 = bf16[16,128,128]{2,1,0:T(8,128)(2,1)} custom-call(s32[640]{0:T(1024)} %plan.1, f32[16,128,128]{2,1,0:T(8,128)} %get-tuple-element.38.own, bf16[8,128,128]{2,1,0:T(8,128)(2,1)} %copy-done.21, bf16[16,128,128]{2,1,0:T(8,128)(2,1)} %copy-done.14), custom_call_target="tpu_custom_call" | custom-call | tf_op jit(solution)/shard_map/hop_7/pallas_call | solution.py:260
  159.4 3.0 %collective-permute-start.35 = (bf16[16,128,128]{2,1,0:T(8,128)(2,1)}, bf16[16,128,128]{2,1,0:T(8,128)(2,1)S(1)}, u32[]{:S(2)}, u32[]{:S(2)}) collective-permute-start(bf16[16,128,128]{2,1,0:T(8,128)(2,1)} %hop_7.1), channel_id=1, source_target_pairs={{0,14},{1,15},{2,0},{3,1},{4,2},{5,3},{6,4},{7,5},{8,6},{9,7},{10,... | collective-permute-start | bytes 1572872 | tf_op jit(solution)/shard_map/ppermute | solution.py:338
  162.3 0.7 copy-done.17
  163.0 0.2 copy-done.15
  163.2 2.5 %hop_1.1 = bf16[16,128,128]{2,1,0:T(8,128)(2,1)} custom-call(s32[640]{0:T(1024)} %plan.1, f32[16,128,128]{2,1,0:T(8,128)} %get-tuple-element.29.own, bf16[8,128,128]{2,1,0:T(8,128)(2,1)} %copy-done.17, bf16[16,128,128]{2,1,0:T(8,128)(2,1)} %copy-done.15), custom_call_target="tpu_custom_call" | custom-call | tf_op jit(solution)/shard_map/hop_1/pallas_call | solution.py:260
  165.7 0.5 collective-permute-start.20
  166.2 7.4 %collective-permute-done.20.arrived = bf16[8,128,128]{2,1,0:T(8,128)(2,1)S(1)} collective-permute-done((bf16[8,128,128]{2,1,0:T(8,128)(2,1)S(1)}, bf16[8,128,128]{2,1,0:T(8,128)(2,1)S(1)}, u32[]{:S(2)}, u32[]{:S(2)}) %collective-permute-start.20) | collective-permute-done | bytes 262176 | tf_op jit(solution)/shard_map/ppermute | solution.py:326
  173.6 2.7 %collective-permute-done.28.passed_a = bf16[16,128,128]{2,1,0:T(8,128)(2,1)S(1)} collective-permute-done((bf16[16,128,128]{2,1,0:T(8,128)(2,1)}, bf16[16,128,128]{2,1,0:T(8,128)(2,1)S(1)}, u32[]{:S(2)}, u32[]{:S(2)}) %collective-permute-start.28) | collective-permute-done | bytes 524320 | tf_op jit(solution)/shard_map/ppermute | solution.py:336
  176.3 0.8 copy-done.11
  177.1 3.3 %last.1 = bf16[2048,256]{1,0:T(8,128)(2,1)} custom-call(s32[640]{0:T(1024)} %plan.1, f32[16,128,128]{2,1,0:T(8,128)} %get-tuple-element.27.own, bf16[8,128,128]{2,1,0:T(8,128)(2,1)} %copy-done.19, bf16[16,128,128]{2,1,0:T(8,128)(2,1)} %copy-done.11, bf16[16,128,128]{2,1,0:T(8,128)(2,1)} %copy-done.10, bf16[128,256]{1,0:T(8,128)(2,1)} %weight.1, ...), custom_call_target="tpu_custom_call" | custom-call | tf_op jit(solution)/shard_map/last/pallas_call | solution.py:279
  (100 shorter events, 0.3 us)
Async XLA Ops:
  0.0 14.5 %collective-permute-start.2 = (bf16[2048,128]{1,0:T(8,128)(2,1)}, bf16[2048,128]{1,0:T(8,128)(2,1)S(1)}, u32[]{:S(2)}, u32[]{:S(2)}) collective-permute-start(bf16[2048,128]{1,0:T(8,128)(2,1)} %refs_1_.1), channel_id=1, source_target_pairs={{0,192},{16,208},{32,224},{48,240},{64,0},{80,16},{96,32},{112,48}... | collective-permute-start | bytes 1572872 | tf_op jit(solution)/shard_map/ppermute | solution.py:290
  3.0 25.8 %collective-permute-start.4 = (bf16[2048,128]{1,0:T(8,128)(2,1)}, bf16[2048,128]{1,0:T(8,128)(2,1)S(1)}, u32[]{:S(2)}, u32[]{:S(2)}) collective-permute-start(bf16[2048,128]{1,0:T(8,128)(2,1)} %refs_1_.1), channel_id=1, source_target_pairs={{0,64},{16,80},{32,96},{48,112},{64,128},{80,144},{96,160},{112,17... | collective-permute-start | bytes 1572872 | tf_op jit(solution)/shard_map/ppermute | solution.py:290
  3.0 26.3 %collective-permute-start.6 = (bf16[2048,128]{1,0:T(8,128)(2,1)}, bf16[2048,128]{1,0:T(8,128)(2,1)S(1)}, u32[]{:S(2)}, u32[]{:S(2)}) collective-permute-start(bf16[2048,128]{1,0:T(8,128)(2,1)} %refs_1_.1), channel_id=1, source_target_pairs={{0,32},{16,48},{32,0},{48,16},{64,96},{80,112},{96,64},{112,80},{1... | collective-permute-start | bytes 1572872 | tf_op jit(solution)/shard_map/ppermute | solution.py:290
  14.5 66.4 %copy-start.3 = (bf16[2048,128]{1,0:T(8,128)(2,1)}, bf16[2048,128]{1,0:T(8,128)(2,1)S(1)}, u32[]{:S(2)}) copy-start(bf16[2048,128]{1,0:T(8,128)(2,1)S(1)} %collective-permute-done.2.refs_3_) | copy-start | bytes 1572868
  14.5 14.9 %collective-permute-start.12 = (bf16[2048,128]{1,0:T(8,128)(2,1)S(1)}, bf16[2048,128]{1,0:T(8,128)(2,1)S(1)}, u32[]{:S(2)}, u32[]{:S(2)}) collective-permute-start(bf16[2048,128]{1,0:T(8,128)(2,1)S(1)} %collective-permute-done.2.refs_3_), channel_id=1, source_target_pairs={{0,32},{16,48},{32,0},{48,16},{64,96},{80,112},{96,64},{112,80},{1... | collective-permute-start | bytes 1572872 | tf_op jit(solution)/shard_map/ppermute | solution.py:290
  15.1 14.8 %collective-permute-start.8 = (bf16[2048,128]{1,0:T(8,128)(2,1)S(1)}, bf16[2048,128]{1,0:T(8,128)(2,1)S(1)}, u32[]{:S(2)}, u32[]{:S(2)}) collective-permute-start(bf16[2048,128]{1,0:T(8,128)(2,1)S(1)} %collective-permute-done.2.refs_3_), channel_id=1, source_target_pairs={{0,192},{16,208},{32,224},{48,240},{64,0},{80,16},{96,32},{112,48}... | collective-permute-start | bytes 1572872 | tf_op jit(solution)/shard_map/ppermute | solution.py:290
  20.0 35.8 %copy-start.30 = (s32[256]{0:T(256)}, s32[256]{0:T(256)S(1)}, u32[]{:S(2)}) copy-start(s32[256]{0:T(256)S(1)} %compare_select_fusion.dest) | copy-start | bytes 3076
  20.0 8.8 %collective-permute-start = (s32[256]{0:T(256)S(1)}, s32[256]{0:T(256)S(1)}, u32[]{:S(2)}, u32[]{:S(2)}) collective-permute-start(s32[256]{0:T(256)S(1)} %compare_select_fusion.dest), channel_id=1, source_target_pairs={{0,1},{1,0},{2,3},{3,2},{4,5},{5,4},{6,7},{7,6},{8,9},{9,8},{10,11... | collective-permute-start | bytes 3080 | tf_op jit(solution)/shard_map/ppermute | solution.py:319
  28.8 26.9 %copy-start.31 = (s32[256]{0:T(256)}, s32[256]{0:T(256)S(1)}, u32[]{:S(2)}) copy-start(s32[256]{0:T(256)S(1)} %collective-permute-done.partner_dest) | copy-start | bytes 3076
  28.8 2.1 %collective-permute-start.1 = (bf16[2048,128]{1,0:T(8,128)(2,1)}, bf16[2048,128]{1,0:T(8,128)(2,1)S(1)}, u32[]{:S(2)}, u32[]{:S(2)}) collective-permute-start(bf16[2048,128]{1,0:T(8,128)(2,1)} %refs_1_.1), channel_id=1, source_target_pairs={{0,16},{16,0},{32,48},{48,32},{64,80},{80,64},{96,112},{112,96},{1... | collective-permute-start | bytes 1572872 | tf_op jit(solution)/shard_map/ppermute | solution.py:290
  28.8 52.2 %copy-start.4 = (bf16[2048,128]{1,0:T(8,128)(2,1)}, bf16[2048,128]{1,0:T(8,128)(2,1)S(1)}, u32[]{:S(2)}) copy-start(bf16[2048,128]{1,0:T(8,128)(2,1)S(1)} %collective-permute-done.4.refs_5_) | copy-start | bytes 1572868
  28.8 3.9 %collective-permute-start.5 = (bf16[2048,128]{1,0:T(8,128)(2,1)S(1)}, bf16[2048,128]{1,0:T(8,128)(2,1)S(1)}, u32[]{:S(2)}, u32[]{:S(2)}) collective-permute-start(bf16[2048,128]{1,0:T(8,128)(2,1)S(1)} %collective-permute-done.4.refs_5_), channel_id=1, source_target_pairs={{0,16},{16,0},{32,48},{48,32},{64,80},{80,64},{96,112},{112,96},{1... | collective-permute-start | bytes 1572872 | tf_op jit(solution)/shard_map/ppermute | solution.py:290
  29.3 51.7 %copy-start.5 = (bf16[2048,128]{1,0:T(8,128)(2,1)}, bf16[2048,128]{1,0:T(8,128)(2,1)S(1)}, u32[]{:S(2)}) copy-start(bf16[2048,128]{1,0:T(8,128)(2,1)S(1)} %collective-permute-done.6.refs_7_) | copy-start | bytes 1572868
  29.3 6.5 %collective-permute-start.3 = (bf16[2048,128]{1,0:T(8,128)(2,1)S(1)}, bf16[2048,128]{1,0:T(8,128)(2,1)S(1)}, u32[]{:S(2)}, u32[]{:S(2)}) collective-permute-start(bf16[2048,128]{1,0:T(8,128)(2,1)S(1)} %collective-permute-done.2.refs_3_), channel_id=1, source_target_pairs={{0,16},{16,0},{32,48},{48,32},{64,80},{80,64},{96,112},{112,96},{1... | collective-permute-start | bytes 1572872 | tf_op jit(solution)/shard_map/ppermute | solution.py:290
  29.4 51.5 %copy-start = (bf16[2048,128]{1,0:T(8,128)(2,1)}, bf16[2048,128]{1,0:T(8,128)(2,1)S(1)}, u32[]{:S(2)}) copy-start(bf16[2048,128]{1,0:T(8,128)(2,1)S(1)} %collective-permute-done.12.refs_13_) | copy-start | bytes 1572868
  29.4 15.5 %collective-permute-start.10 = (bf16[2048,128]{1,0:T(8,128)(2,1)S(1)}, bf16[2048,128]{1,0:T(8,128)(2,1)S(1)}, u32[]{:S(2)}, u32[]{:S(2)}) collective-permute-start(bf16[2048,128]{1,0:T(8,128)(2,1)S(1)} %collective-permute-done.6.refs_7_), channel_id=1, source_target_pairs={{0,64},{16,80},{32,96},{48,112},{64,128},{80,144},{96,160},{112,17... | collective-permute-start | bytes 1572872 | tf_op jit(solution)/shard_map/ppermute | solution.py:290
  29.8 51.2 %copy-start.2 = (bf16[2048,128]{1,0:T(8,128)(2,1)}, bf16[2048,128]{1,0:T(8,128)(2,1)S(1)}, u32[]{:S(2)}) copy-start(bf16[2048,128]{1,0:T(8,128)(2,1)S(1)} %collective-permute-done.8.refs_9_) | copy-start | bytes 1572868
  29.8 15.1 %collective-permute-start.7 = (bf16[2048,128]{1,0:T(8,128)(2,1)S(1)}, bf16[2048,128]{1,0:T(8,128)(2,1)S(1)}, u32[]{:S(2)}, u32[]{:S(2)}) collective-permute-start(bf16[2048,128]{1,0:T(8,128)(2,1)S(1)} %collective-permute-done.6.refs_7_), channel_id=1, source_target_pairs={{0,16},{16,0},{32,48},{48,32},{64,80},{80,64},{96,112},{112,96},{1... | collective-permute-start | bytes 1572872 | tf_op jit(solution)/shard_map/ppermute | solution.py:290
  30.9 14.1 %copy-start.6 = (bf16[2048,128]{1,0:T(8,128)(2,1)}, bf16[2048,128]{1,0:T(8,128)(2,1)S(1)}, u32[]{:S(2)}) copy-start(bf16[2048,128]{1,0:T(8,128)(2,1)S(1)} %collective-permute-done.1.refs_2_) | copy-start | bytes 1572868
  30.9 14.7 %collective-permute-start.18 = (bf16[672,128]{1,0:T(8,128)(2,1)S(1)}, bf16[672,128]{1,0:T(8,128)(2,1)S(1)}, u32[]{:S(2)}, u32[]{:S(2)}) collective-permute-start(bf16[672,128]{1,0:T(8,128)(2,1)S(1)} %slice.14), channel_id=1, source_target_pairs={{0,32},{16,48},{32,0},{48,16},{64,96},{80,112},{96,64},{112,80},{1... | collective-permute-start | bytes 516104 | tf_op jit(solution)/shard_map/ppermute | solution.py:290
  32.7 12.8 %copy-start.7 = (bf16[2048,128]{1,0:T(8,128)(2,1)}, bf16[2048,128]{1,0:T(8,128)(2,1)S(1)}, u32[]{:S(2)}) copy-start(bf16[2048,128]{1,0:T(8,128)(2,1)S(1)} %collective-permute-done.5.refs_6_) | copy-start | bytes 1572868
  32.7 13.1 %collective-permute-start.14 = (bf16[688,128]{1,0:T(8,128)(2,1)S(1)}, bf16[688,128]{1,0:T(8,128)(2,1)S(1)}, u32[]{:S(2)}, u32[]{:S(2)}) collective-permute-start(bf16[688,128]{1,0:T(8,128)(2,1)S(1)} %slice.12), channel_id=1, source_target_pairs={{0,192},{16,208},{32,224},{48,240},{64,0},{80,16},{96,32},{112,48}... | collective-permute-start | bytes 528392 | tf_op jit(solution)/shard_map/ppermute | solution.py:290
  35.8 9.8 %copy-start.8 = (bf16[2048,128]{1,0:T(8,128)(2,1)}, bf16[2048,128]{1,0:T(8,128)(2,1)S(1)}, u32[]{:S(2)}) copy-start(bf16[2048,128]{1,0:T(8,128)(2,1)S(1)} %collective-permute-done.3.refs_4_) | copy-start | bytes 1572868
  35.8 45.1 %collective-permute-start.13 = (bf16[2048,128]{1,0:T(8,128)(2,1)S(1)}, bf16[2048,128]{1,0:T(8,128)(2,1)}, u32[]{:S(2)}, u32[]{:S(2)}) collective-permute-start(bf16[2048,128]{1,0:T(8,128)(2,1)S(1)} %collective-permute-done.12.refs_13_), channel_id=1, source_target_pairs={{0,16},{16,0},{32,48},{48,32},{64,80},{80,64},{96,112},{112,96},{1... | collective-permute-start | bytes 1572872 | tf_op jit(solution)/shard_map/ppermute | solution.py:290
  45.0 36.0 %copy-start.1 = (bf16[2048,128]{1,0:T(8,128)(2,1)}, bf16[2048,128]{1,0:T(8,128)(2,1)S(1)}, u32[]{:S(2)}) copy-start(bf16[2048,128]{1,0:T(8,128)(2,1)S(1)} %collective-permute-done.10.refs_11_) | copy-start | bytes 1572868
  45.0 36.0 %collective-permute-start.9 = (bf16[2048,128]{1,0:T(8,128)(2,1)S(1)}, bf16[2048,128]{1,0:T(8,128)(2,1)}, u32[]{:S(2)}, u32[]{:S(2)}) collective-permute-start(bf16[2048,128]{1,0:T(8,128)(2,1)S(1)} %collective-permute-done.8.refs_9_), channel_id=1, source_target_pairs={{0,16},{16,0},{32,48},{48,32},{64,80},{80,64},{96,112},{112,96},{1... | collective-permute-start | bytes 1572872 | tf_op jit(solution)/shard_map/ppermute | solution.py:290
  45.0 0.8 copy-start.9
  45.0 35.9 %collective-permute-start.11 = (bf16[2048,128]{1,0:T(8,128)(2,1)S(1)}, bf16[2048,128]{1,0:T(8,128)(2,1)}, u32[]{:S(2)}, u32[]{:S(2)}) collective-permute-start(bf16[2048,128]{1,0:T(8,128)(2,1)S(1)} %collective-permute-done.10.refs_11_), channel_id=1, source_target_pairs={{0,16},{16,0},{32,48},{48,32},{64,80},{80,64},{96,112},{112,96},{1... | collective-permute-start | bytes 1572872 | tf_op jit(solution)/shard_map/ppermute | solution.py:290
  45.8 8.1 %copy-start.28 = (bf16[672,128]{1,0:T(8,128)(2,1)}, bf16[672,128]{1,0:T(8,128)(2,1)S(1)}, u32[]{:S(2)}) copy-start(bf16[672,128]{1,0:T(8,128)(2,1)S(1)} %collective-permute-done.18.refs_19_) | copy-start | bytes 516100
  45.8 8.0 %collective-permute-start.16 = (bf16[688,128]{1,0:T(8,128)(2,1)S(1)}, bf16[688,128]{1,0:T(8,128)(2,1)S(1)}, u32[]{:S(2)}, u32[]{:S(2)}) collective-permute-start(bf16[688,128]{1,0:T(8,128)(2,1)S(1)} %slice.13), channel_id=1, source_target_pairs={{0,64},{16,80},{32,96},{48,112},{64,128},{80,144},{96,160},{112,17... | collective-permute-start | bytes 528392 | tf_op jit(solution)/shard_map/ppermute | solution.py:290
  45.8 35.2 %copy-start.26 = (bf16[688,128]{1,0:T(8,128)(2,1)}, bf16[688,128]{1,0:T(8,128)(2,1)S(1)}, u32[]{:S(2)}) copy-start(bf16[688,128]{1,0:T(8,128)(2,1)S(1)} %collective-permute-done.14.refs_15_) | copy-start | bytes 528388
  45.8 8.0 %collective-permute-start.19 = (bf16[672,128]{1,0:T(8,128)(2,1)S(1)}, bf16[672,128]{1,0:T(8,128)(2,1)S(1)}, u32[]{:S(2)}, u32[]{:S(2)}) collective-permute-start(bf16[672,128]{1,0:T(8,128)(2,1)S(1)} %collective-permute-done.18.refs_19_), channel_id=1, source_target_pairs={{0,16},{16,0},{32,48},{48,32},{64,80},{80,64},{96,112},{112,96},{1... | collective-permute-start | bytes 516104 | tf_op jit(solution)/shard_map/ppermute | solution.py:290
  53.9 27.2 %copy-start.27 = (bf16[688,128]{1,0:T(8,128)(2,1)}, bf16[688,128]{1,0:T(8,128)(2,1)S(1)}, u32[]{:S(2)}) copy-start(bf16[688,128]{1,0:T(8,128)(2,1)S(1)} %collective-permute-done.16.refs_17_) | copy-start | bytes 528388
  53.9 27.0 %collective-permute-start.15 = (bf16[688,128]{1,0:T(8,128)(2,1)S(1)}, bf16[688,128]{1,0:T(8,128)(2,1)}, u32[]{:S(2)}, u32[]{:S(2)}) collective-permute-start(bf16[688,128]{1,0:T(8,128)(2,1)S(1)} %collective-permute-done.14.refs_15_), channel_id=1, source_target_pairs={{0,16},{16,0},{32,48},{48,32},{64,80},{80,64},{96,112},{112,96},{1... | collective-permute-start | bytes 528392 | tf_op jit(solution)/shard_map/ppermute | solution.py:290
  54.6 26.3 %collective-permute-start.17 = (bf16[688,128]{1,0:T(8,128)(2,1)S(1)}, bf16[688,128]{1,0:T(8,128)(2,1)}, u32[]{:S(2)}, u32[]{:S(2)}) collective-permute-start(bf16[688,128]{1,0:T(8,128)(2,1)S(1)} %collective-permute-done.16.refs_17_), channel_id=1, source_target_pairs={{0,16},{16,0},{32,48},{48,32},{64,80},{80,64},{96,112},{112,96},{1... | collective-permute-start | bytes 528392 | tf_op jit(solution)/shard_map/ppermute | solution.py:290
  90.6 10.7 %collective-permute-start.24 = (bf16[8,128,128]{2,1,0:T(8,128)(2,1)}, bf16[8,128,128]{2,1,0:T(8,128)(2,1)S(1)}, u32[]{:S(2)}, u32[]{:S(2)}) collective-permute-start(bf16[8,128,128]{2,1,0:T(8,128)(2,1)} %get-tuple-element.36), channel_id=1, source_target_pairs={{0,1},{1,0},{2,3},{3,2},{4,5},{5,4},{6,7},{7,6},{8,9},{9,8},{10,11... | collective-permute-start | bytes 786440 | tf_op jit(solution)/shard_map/ppermute | solution.py:326
  93.0 18.9 %collective-permute-start.31 = (bf16[8,128,128]{2,1,0:T(8,128)(2,1)}, bf16[8,128,128]{2,1,0:T(8,128)(2,1)S(1)}, u32[]{:S(2)}, u32[]{:S(2)}) collective-permute-start(bf16[8,128,128]{2,1,0:T(8,128)(2,1)} %get-tuple-element.43), channel_id=1, source_target_pairs={{0,1},{1,0},{2,3},{3,2},{4,5},{5,4},{6,7},{7,6},{8,9},{9,8},{10,11... | collective-permute-start | bytes 786440 | tf_op jit(solution)/shard_map/ppermute | solution.py:326
  94.2 14.3 %copy-start.37 = (bf16[8,128,128]{2,1,0:T(8,128)(2,1)S(1)}, bf16[8,128,128]{2,1,0:T(8,128)(2,1)}, u32[]{:S(2)}) copy-start(bf16[8,128,128]{2,1,0:T(8,128)(2,1)} %get-tuple-element.34) | copy-start | bytes 786436
  94.2 30.8 %copy-start.36 = (bf16[8,128,128]{2,1,0:T(8,128)(2,1)S(1)}, bf16[8,128,128]{2,1,0:T(8,128)(2,1)}, u32[]{:S(2)}) copy-start(bf16[8,128,128]{2,1,0:T(8,128)(2,1)} %get-tuple-element.41) | copy-start | bytes 786436
  94.2 31.6 %copy-start.35 = (bf16[8,128,128]{2,1,0:T(8,128)(2,1)S(1)}, bf16[8,128,128]{2,1,0:T(8,128)(2,1)}, u32[]{:S(2)}) copy-start(bf16[8,128,128]{2,1,0:T(8,128)(2,1)} %get-tuple-element.32) | copy-start | bytes 786436
  100.7 45.1 %copy-start.34 = (bf16[8,128,128]{2,1,0:T(8,128)(2,1)S(1)}, bf16[8,128,128]{2,1,0:T(8,128)(2,1)}, u32[]{:S(2)}) copy-start(bf16[8,128,128]{2,1,0:T(8,128)(2,1)} %get-tuple-element.39) | copy-start | bytes 786436
  100.7 46.0 %copy-start.33 = (bf16[8,128,128]{2,1,0:T(8,128)(2,1)S(1)}, bf16[8,128,128]{2,1,0:T(8,128)(2,1)}, u32[]{:S(2)}) copy-start(bf16[8,128,128]{2,1,0:T(8,128)(2,1)} %get-tuple-element.30) | copy-start | bytes 786436
  100.7 65.0 %copy-start.32 = (bf16[8,128,128]{2,1,0:T(8,128)(2,1)S(1)}, bf16[8,128,128]{2,1,0:T(8,128)(2,1)}, u32[]{:S(2)}) copy-start(bf16[8,128,128]{2,1,0:T(8,128)(2,1)} %get-tuple-element.28) | copy-start | bytes 786436
  104.3 10.9 %collective-permute-start.32 = (bf16[8,128,128]{2,1,0:T(8,128)(2,1)}, bf16[8,128,128]{2,1,0:T(8,128)(2,1)S(1)}, u32[]{:S(2)}, u32[]{:S(2)}) collective-permute-start(bf16[8,128,128]{2,1,0:T(8,128)(2,1)} %get-tuple-element.44), channel_id=1, source_target_pairs={{0,14},{1,15},{2,0},{3,1},{4,2},{5,3},{6,4},{7,5},{8,6},{9,7},{10,... | collective-permute-start | bytes 786440 | tf_op jit(solution)/shard_map/ppermute | solution.py:332
  108.6 13.3 %collective-permute-start.23 = (bf16[8,128,128]{2,1,0:T(8,128)(2,1)S(1)}, bf16[8,128,128]{2,1,0:T(8,128)(2,1)S(1)}, u32[]{:S(2)}, u32[]{:S(2)}) collective-permute-start(bf16[8,128,128]{2,1,0:T(8,128)(2,1)S(1)} %copy-done.37), channel_id=1, source_target_pairs={{0,1},{1,0},{2,3},{3,2},{4,5},{5,4},{6,7},{7,6},{8,9},{9,8},{10,11... | collective-permute-start | bytes 786440 | tf_op jit(solution)/shard_map/ppermute | solution.py:326
  111.8 10.0 %collective-permute-start.25 = (bf16[8,128,128]{2,1,0:T(8,128)(2,1)}, bf16[8,128,128]{2,1,0:T(8,128)(2,1)S(1)}, u32[]{:S(2)}, u32[]{:S(2)}) collective-permute-start(bf16[8,128,128]{2,1,0:T(8,128)(2,1)} %get-tuple-element.37), channel_id=1, source_target_pairs={{0,2},{1,3},{2,4},{3,5},{4,6},{5,7},{6,8},{7,9},{8,10},{9,11},{10,... | collective-permute-start | bytes 786440 | tf_op jit(solution)/shard_map/ppermute | solution.py:332
  111.8 3.4 %copy-start.22 = (bf16[8,128,128]{2,1,0:T(8,128)(2,1)}, bf16[8,128,128]{2,1,0:T(8,128)(2,1)S(1)}, u32[]{:S(2)}) copy-start(bf16[8,128,128]{2,1,0:T(8,128)(2,1)S(1)} %collective-permute-done.31.arrived) | copy-start | bytes 786436
  118.3 17.4 %collective-permute-start.33 = (bf16[16,128,128]{2,1,0:T(8,128)(2,1)}, bf16[16,128,128]{2,1,0:T(8,128)(2,1)S(1)}, u32[]{:S(2)}, u32[]{:S(2)}) collective-permute-start(bf16[16,128,128]{2,1,0:T(8,128)(2,1)} %hop_5.1), channel_id=1, source_target_pairs={{0,14},{1,15},{2,0},{3,1},{4,2},{5,3},{6,4},{7,5},{8,6},{9,7},{10,... | collective-permute-start | bytes 1572872 | tf_op jit(solution)/shard_map/ppermute | solution.py:338
  125.0 17.4 %collective-permute-start.26 = (bf16[16,128,128]{2,1,0:T(8,128)(2,1)}, bf16[16,128,128]{2,1,0:T(8,128)(2,1)S(1)}, u32[]{:S(2)}, u32[]{:S(2)}) collective-permute-start(bf16[16,128,128]{2,1,0:T(8,128)(2,1)} %hop_3.1), channel_id=1, source_target_pairs={{0,2},{1,3},{2,4},{3,5},{4,6},{5,7},{6,8},{7,9},{8,10},{9,11},{10,... | collective-permute-start | bytes 1572872 | tf_op jit(solution)/shard_map/ppermute | solution.py:336
  125.0 10.7 %collective-permute-start.30 = (bf16[8,128,128]{2,1,0:T(8,128)(2,1)S(1)}, bf16[8,128,128]{2,1,0:T(8,128)(2,1)S(1)}, u32[]{:S(2)}, u32[]{:S(2)}) collective-permute-start(bf16[8,128,128]{2,1,0:T(8,128)(2,1)S(1)} %copy-done.36), channel_id=1, source_target_pairs={{0,1},{1,0},{2,3},{3,2},{4,5},{5,4},{6,7},{7,6},{8,9},{9,8},{10,11... | collective-permute-start | bytes 786440 | tf_op jit(solution)/shard_map/ppermute | solution.py:326
  125.8 16.5 %collective-permute-start.22 = (bf16[8,128,128]{2,1,0:T(8,128)(2,1)S(1)}, bf16[8,128,128]{2,1,0:T(8,128)(2,1)S(1)}, u32[]{:S(2)}, u32[]{:S(2)}) collective-permute-start(bf16[8,128,128]{2,1,0:T(8,128)(2,1)S(1)} %copy-done.35), channel_id=1, source_target_pairs={{0,1},{1,0},{2,3},{3,2},{4,5},{5,4},{6,7},{7,6},{8,9},{9,8},{10,11... | collective-permute-start | bytes 786440 | tf_op jit(solution)/shard_map/ppermute | solution.py:326
  135.7 0.9 copy-start.12
  139.1 16.9 %collective-permute-start.34 = (bf16[16,128,128]{2,1,0:T(8,128)(2,1)}, bf16[16,128,128]{2,1,0:T(8,128)(2,1)S(1)}, u32[]{:S(2)}, u32[]{:S(2)}) collective-permute-start(bf16[16,128,128]{2,1,0:T(8,128)(2,1)} %hop_6.1), channel_id=1, source_target_pairs={{0,14},{1,15},{2,0},{3,1},{4,2},{5,3},{6,4},{7,5},{8,6},{9,7},{10,... | collective-permute-start | bytes 1572872 | tf_op jit(solution)/shard_map/ppermute | solution.py:338
  142.4 0.9 copy-start.13
  145.7 16.6 %collective-permute-start.27 = (bf16[16,128,128]{2,1,0:T(8,128)(2,1)}, bf16[16,128,128]{2,1,0:T(8,128)(2,1)S(1)}, u32[]{:S(2)}, u32[]{:S(2)}) collective-permute-start(bf16[16,128,128]{2,1,0:T(8,128)(2,1)} %hop_2.1), channel_id=1, source_target_pairs={{0,2},{1,3},{2,4},{3,5},{4,6},{5,7},{6,8},{7,9},{8,10},{9,11},{10,... | collective-permute-start | bytes 1572872 | tf_op jit(solution)/shard_map/ppermute | solution.py:336
  145.7 10.2 %collective-permute-start.29 = (bf16[8,128,128]{2,1,0:T(8,128)(2,1)S(1)}, bf16[8,128,128]{2,1,0:T(8,128)(2,1)S(1)}, u32[]{:S(2)}, u32[]{:S(2)}) collective-permute-start(bf16[8,128,128]{2,1,0:T(8,128)(2,1)S(1)} %copy-done.34), channel_id=1, source_target_pairs={{0,1},{1,0},{2,3},{3,2},{4,5},{5,4},{6,7},{7,6},{8,9},{9,8},{10,11... | collective-permute-start | bytes 786440 | tf_op jit(solution)/shard_map/ppermute | solution.py:326
  146.6 15.7 %collective-permute-start.21 = (bf16[8,128,128]{2,1,0:T(8,128)(2,1)S(1)}, bf16[8,128,128]{2,1,0:T(8,128)(2,1)S(1)}, u32[]{:S(2)}, u32[]{:S(2)}) collective-permute-start(bf16[8,128,128]{2,1,0:T(8,128)(2,1)S(1)} %copy-done.33), channel_id=1, source_target_pairs={{0,1},{1,0},{2,3},{3,2},{4,5},{5,4},{6,7},{7,6},{8,9},{9,8},{10,11... | collective-permute-start | bytes 786440 | tf_op jit(solution)/shard_map/ppermute | solution.py:326
  156.0 0.9 copy-start.14
  159.4 14.2 %collective-permute-start.35 = (bf16[16,128,128]{2,1,0:T(8,128)(2,1)}, bf16[16,128,128]{2,1,0:T(8,128)(2,1)S(1)}, u32[]{:S(2)}, u32[]{:S(2)}) collective-permute-start(bf16[16,128,128]{2,1,0:T(8,128)(2,1)} %hop_7.1), channel_id=1, source_target_pairs={{0,14},{1,15},{2,0},{3,1},{4,2},{5,3},{6,4},{7,5},{8,6},{9,7},{10,... | collective-permute-start | bytes 1572872 | tf_op jit(solution)/shard_map/ppermute | solution.py:338
  162.3 0.9 copy-start.15
  165.7 10.6 %collective-permute-start.28 = (bf16[16,128,128]{2,1,0:T(8,128)(2,1)}, bf16[16,128,128]{2,1,0:T(8,128)(2,1)S(1)}, u32[]{:S(2)}, u32[]{:S(2)}) collective-permute-start(bf16[16,128,128]{2,1,0:T(8,128)(2,1)} %hop_1.1), channel_id=1, source_target_pairs={{0,2},{1,3},{2,4},{3,5},{4,6},{5,7},{6,8},{7,9},{8,10},{9,11},{10,... | collective-permute-start | bytes 1572872 | tf_op jit(solution)/shard_map/ppermute | solution.py:336
  165.7 7.9 %collective-permute-start.20 = (bf16[8,128,128]{2,1,0:T(8,128)(2,1)S(1)}, bf16[8,128,128]{2,1,0:T(8,128)(2,1)S(1)}, u32[]{:S(2)}, u32[]{:S(2)}) collective-permute-start(bf16[8,128,128]{2,1,0:T(8,128)(2,1)S(1)} %copy-done.32), channel_id=1, source_target_pairs={{0,1},{1,0},{2,3},{3,2},{4,5},{5,4},{6,7},{7,6},{8,9},{9,8},{10,11... | collective-permute-start | bytes 786440 | tf_op jit(solution)/shard_map/ppermute | solution.py:326
  173.6 2.7 %copy-start.19 = (bf16[8,128,128]{2,1,0:T(8,128)(2,1)}, bf16[8,128,128]{2,1,0:T(8,128)(2,1)S(1)}, u32[]{:S(2)}) copy-start(bf16[8,128,128]{2,1,0:T(8,128)(2,1)S(1)} %collective-permute-done.20.arrived) | copy-start | bytes 786436
  173.6 2.7 %copy-start.10 = (bf16[16,128,128]{2,1,0:T(8,128)(2,1)}, bf16[16,128,128]{2,1,0:T(8,128)(2,1)S(1)}, u32[]{:S(2)}) copy-start(bf16[16,128,128]{2,1,0:T(8,128)(2,1)S(1)} %collective-permute-done.35.passed_b) | copy-start | bytes 1572868
  (10 other events, 7.3 us)

commit v2 on v0

v2 whole, which is shorter than its diff:
```python
import functools

import jax
import jax.numpy as jnp
from jax import lax
from jax.experimental import pallas as pl
from jax.experimental.pallas import tpu as pltpu
from jax.sharding import PartitionSpec as P

TILE = 128
TPD = 16
SLOTS = 256
NY, NXLO, NCORE = 4, 2, 2
NZ, NXHI = 8, 2
ROWS = TPD * TILE
HALF_SLOTS = 8
OWN_BLOCKS = NZ * TPD
OTHER_BLOCKS = NZ * HALF_SLOTS
TRASH = OWN_BLOCKS
GROUP = 8
WIDTH = 384
THIRDS = (688, 688, 672)

VMEM = pltpu.VMEM
SMEM_SPEC = pl.BlockSpec(memory_space=pltpu.SMEM)
VMEM_SPEC = pl.BlockSpec(memory_space=pltpu.VMEM)
ANY_SPEC = pl.BlockSpec(memory_space=pl.ANY)


def row_perm(change):
    pairs = []
    for y in range(NY):
        for x in range(NXLO):
            for k in range(NCORE):
                ty, tx, tk = change(y, x, k)
                pairs.append(((y * NXLO + x) * NCORE + k, (ty % NY * NXLO + tx) * NCORE + tk))
    return pairs


FROM_UP = row_perm(lambda y, x, k: (y - 1, x, k))
FROM_DOWN = row_perm(lambda y, x, k: (y + 1, x, k))
FROM_SIDE = row_perm(lambda y, x, k: (y, 1 - x, k))
FROM_CORE = row_perm(lambda y, x, k: (y, x, 1 - k))
Z_PLUS = [(z * NXHI + x, (z + 1) % NZ * NXHI + x) for z in range(NZ) for x in range(NXHI)]
Z_MINUS = [(z * NXHI + x, (z - 1) % NZ * NXHI + x) for z in range(NZ) for x in range(NXHI)]
X_FLIP = [(z * NXHI + x, z * NXHI + 1 - x) for z in range(NZ) for x in range(NXHI)]


def call(kernel, name, **kwargs):
    return pl.pallas_call(
        kernel,
        name=name,
        cost_estimate=pl.CostEstimate(flops=0, bytes_accessed=0, transcendentals=0),
        compiler_params=pltpu.CompilerParams(vmem_limit_bytes=16 << 20),
        **kwargs,
    )


def keep(array):
    return pltpu.with_memory_space_constraint(array, pltpu.VMEM)


def iota(shape, dim):
    return lax.broadcasted_iota(jnp.int32, shape, dim)


def to_column(row):
    n = row.shape[1]
    square = jnp.broadcast_to(row, (n, n))
    return jnp.sum(jnp.where(iota((n, n), 0) == iota((n, n), 1), square, 0.0), 1, keepdims=True)


def to_row(column):
    n = column.shape[0]
    square = jnp.broadcast_to(column, (n, n))
    return jnp.sum(jnp.where(iota((n, n), 0) == iota((n, n), 1), square, 0.0), 0, keepdims=True)


def split_dest(block, my_z):
    block = jnp.maximum(block, 0)
    away = ((block // (NXHI * TPD)) - my_z) & (NZ - 1)
    return away, (block // TPD) & (NXHI - 1), block & (TPD - 1)


def slots_of(key, chosen):
    hit = (iota((OWN_BLOCKS, SLOTS), 0) == key) & chosen
    touched = jnp.max(jnp.where(hit, 1.0, 0.0), axis=1, keepdims=True)
    a, b = iota((OWN_BLOCKS, OWN_BLOCKS), 0), iota((OWN_BLOCKS, OWN_BLOCKS), 1)
    before = (b < a) & (b // TPD == a // TPD)
    rank = jnp.sum(jnp.where(before, to_row(touched), 0.0), axis=1, keepdims=True)
    return hit, touched, rank


def listed(chosen, value):
    mark = to_column(jnp.where(chosen, 1.0, 0.0))
    earlier = iota((SLOTS, SLOTS), 0) < iota((SLOTS, SLOTS), 1)
    at = to_column(jnp.sum(jnp.where(earlier, mark, 0.0), axis=0, keepdims=True))
    count = jnp.sum(mark)
    place = iota((SLOTS, WIDTH), 1).astype(jnp.float32)
    value = to_column(value.astype(jnp.float32))
    row = jnp.sum(jnp.where((at == place) & (mark > 0), value, 0.0), axis=0, keepdims=True)
    empty = iota((1, WIDTH), 1).astype(jnp.float32) >= count
    return jnp.where(empty, float(TRASH << 16), row).astype(jnp.int32), count


def plan_kernel(where, dest, source, partner_dest, plan):
    my_y, my_x, my_k, my_z, my_xhi = (where[i] for i in range(5))
    block, from_block = dest[...], source[...]
    row = from_block // TPD
    rel = ((row // (NXLO * NCORE)) - my_y) & (NY - 1)
    rel = rel * NXLO + (((row // NCORE) - my_x) & (NXLO - 1))
    rel = rel * NCORE + ((row - my_k) & (NCORE - 1))
    rel = rel * TPD + (from_block & (TPD - 1))
    away, half, inner = split_dest(block, my_z)
    key = away * TPD + inner
    is_own = (block >= 0) & (half == my_xhi)
    is_other = (block >= 0) & (half != my_xhi)
    tile = iota((1, SLOTS), 1) + rel * 256
    hit, _, rank = slots_of(key, is_other)
    slot = jnp.sum(jnp.where(hit, rank, 0.0), axis=0, keepdims=True).astype(jnp.int32)
    other, n_other = listed(is_other, tile + (away * HALF_SLOTS + slot) * 65536)
    own, n_own = listed(is_own, tile + key * 65536)
    away, half, inner = split_dest(partner_dest[...], my_z)
    sent = (partner_dest[...] >= 0) & (half == my_xhi)
    _, touched, rank = slots_of(away * TPD + inner, sent)
    slot = to_row(jnp.where(touched > 0, rank, float(HALF_SLOTS))).astype(jnp.int32)
    plan[0:1, :] = other
    plan[1:2, :] = own
    plan[2:3, 0:OWN_BLOCKS] = slot
    lane = iota((1, WIDTH - OWN_BLOCKS), 1)
    counts = jnp.where(lane == 0, n_other, n_own).astype(jnp.int32)
    plan[2:3, OWN_BLOCKS:] = (counts + (GROUP - 1)) // GROUP


def make_plan(where, dest, source, partner_dest):
    return call(
        plan_kernel,
        "plan",
        out_shape=jax.ShapeDtypeStruct((8, WIDTH), jnp.int32),
        in_specs=[SMEM_SPEC] + [VMEM_SPEC] * 3,
        out_specs=VMEM_SPEC,
    )(where, dest, source, partner_dest)


def add_products(plan, which, tiles, feats, acc):
    def one_group(g, _):
        entries = [plan[which, g * GROUP + i] for i in range(GROUP)]
        products = [
            jnp.dot(
                tiles[e & 255],
                feats[pl.ds(pl.multiple_of(((e >> 8) & 255) * TILE, TILE), TILE), :],
                preferred_element_type=jnp.float32,
            )
            for e in entries
        ]
        for e, product in zip(entries, products):
            acc[e >> 16] += product
        return 0

    lax.fori_loop(0, plan[2, OWN_BLOCKS + which], one_group, 0)


def clear_blocks(acc, n):
    def clear(i, _):
        acc[i] = jnp.zeros(acc.shape[1:], acc.dtype)
        return 0

    lax.fori_loop(0, n, clear, 0, unroll=4)


def load_tiles_kernel(tiles_hbm, tiles, sem):
    copy = pltpu.make_async_copy(tiles_hbm, tiles, sem)
    copy.start()
    copy.wait()


def load_tiles(tile_set):
    return call(
        load_tiles_kernel,
        "load_tiles",
        out_shape=VMEM(tile_set.shape, tile_set.dtype),
        in_specs=[ANY_SPEC],
        out_specs=VMEM_SPEC,
        scratch_shapes=[pltpu.SemaphoreType.DMA(())],
    )(tile_set)


def load_feats_kernel(pieces, has_base, *refs):
    feats = refs[-1]
    for (at, n), ref in zip(pieces, refs[has_base:]):
        feats[pl.ds(at, n), :] = ref[...]


def load_feats(base, pieces):
    places = tuple((at, array.shape[0]) for at, array in pieces)
    arrays = [array for _, array in pieces]
    has_base = base is not None
    return call(
        functools.partial(load_feats_kernel, places, has_base),
        "load_feats",
        out_shape=VMEM((SLOTS * TILE, arrays[0].shape[1]), arrays[0].dtype),
        in_specs=[VMEM_SPEC] * (has_base + len(arrays)),
        out_specs=VMEM_SPEC,
        input_output_aliases={0: 0} if has_base else {},
    )(*([keep(base)] if has_base else []), *arrays)


def other_kernel(plan, tiles, feats, *refs):
    sends, acc = refs[:NZ], refs[NZ]
    clear_blocks(acc, OTHER_BLOCKS)
    add_products(plan, 0, tiles, feats, acc)
    for away, send in enumerate(sends):
        send[...] = acc[pl.ds(away * HALF_SLOTS, HALF_SLOTS)].astype(send.dtype)


def other_half(plan, tiles, feats):
    width = feats.shape[1]
    return call(
        other_kernel,
        "other_half",
        out_shape=[VMEM((HALF_SLOTS, TILE, width), jnp.bfloat16)] * NZ,
        in_specs=[SMEM_SPEC, VMEM_SPEC, VMEM_SPEC],
        out_specs=[VMEM_SPEC] * NZ,
        scratch_shapes=[VMEM((TRASH + 1, TILE, width), jnp.float32)],
    )(plan, keep(tiles), keep(feats))


def own_kernel(plan, tiles, feats, acc):
    clear_blocks(acc, OWN_BLOCKS)
    add_products(plan, 1, tiles, feats, acc)


def own_half(plan, tiles, feats):
    return call(
        own_kernel,
        "own_half",
        out_shape=VMEM((TRASH + 1, TILE, feats.shape[1]), jnp.float32),
        in_specs=[SMEM_SPEC, VMEM_SPEC, VMEM_SPEC],
        out_specs=VMEM_SPEC,
    )(plan, keep(tiles), keep(feats))


def merged(away, plan, own, arrived, passed, i):
    total = own[away * TPD + i]
    for ref, at in passed:
        if at <= i < at + ref.shape[0]:
            total += ref[i - at].astype(jnp.float32)
    slot = plan[2, away * TPD + i]
    seen = (slot < HALF_SLOTS).astype(jnp.float32)
    return total + arrived[jnp.minimum(slot, HALF_SLOTS - 1)].astype(jnp.float32) * seen


def hop_kernel(away, pass_at, cuts, plan, own, arrived, *refs):
    passed = list(zip(refs[: len(pass_at)], pass_at))
    for out, (at, n) in zip(refs[len(pass_at) :], cuts):
        for i in range(n):
            out[i] = merged(away, plan, own, arrived, passed, at + i).astype(out.dtype)


def hop(away, plan, own, arrived, passed, pass_at, cuts):
    width = own.shape[-1]
    return call(
        functools.partial(hop_kernel, away, pass_at, cuts),
        f"hop_{away}",
        out_shape=[VMEM((n, TILE, width), jnp.bfloat16) for _, n in cuts],
        in_specs=[SMEM_SPEC] + [VMEM_SPEC] * (2 + len(passed)),
        out_specs=[VMEM_SPEC] * len(cuts),
    )(plan, keep(own), arrived, *passed)


def last_kernel(plan, own, arrived, passed_a, passed_b, weight, bias, out):
    passed = [(passed_a, 0), (passed_b, 0)]
    for i in range(TPD):
        total = merged(0, plan, own, arrived, passed, i).astype(jnp.bfloat16)
        hidden = jnp.dot(total, weight[...], preferred_element_type=jnp.float32) + bias[...]
        out[pl.ds(i * TILE, TILE), :] = jnp.maximum(hidden, 0.0).astype(out.dtype)


def last(plan, own, arrived, passed_a, passed_b, weight, bias):
    return call(
        last_kernel,
        "last",
        out_shape=jax.ShapeDtypeStruct((ROWS, weight.shape[1]), jnp.bfloat16),
        in_specs=[SMEM_SPEC] + [VMEM_SPEC] * 6,
        out_specs=VMEM_SPEC,
    )(plan, keep(own), arrived, passed_a, passed_b, weight, bias)


def send(array, perm):
    return lax.ppermute(array, "row", perm)


def both_cores(y, x, array, first=0):
    at = ((y * NXLO + x) * NCORE) * ROWS + first
    return [(at, array), (at + ROWS, send(array, FROM_CORE))]


def on_device(node_feats, tile_vals, tile_dest, tile_source, tile_count, weight, out_bias):
    row, col = lax.axis_index("row"), lax.axis_index("col")
    where = jnp.stack(
        [row // (NXLO * NCORE), row // NCORE % NXLO, row % NCORE, col // NXHI, col % NXHI]
    ).astype(jnp.int32)
    slots = jnp.arange(SLOTS, dtype=jnp.int32)[None, :]
    dest = jnp.where(slots < tile_count[0, 0], tile_dest[0], -1)
    partner_dest = lax.ppermute(dest, "col", X_FLIP)
    up, down, side = (send(node_feats, p) for p in (FROM_UP, FROM_DOWN, FROM_SIDE))
    own_pieces = both_cores(0, 0, node_feats)
    plan = make_plan(where, dest, tile_source[0], partner_dest)
    tiles = load_tiles(tile_vals[0, 0])
    up, down, side, plan = lax.optimization_barrier((up, down, side, plan))
    far, down_side, up_side = send(up, FROM_UP), send(side, FROM_DOWN), send(up, FROM_SIDE)
    pieces = both_cores(1, 0, up) + both_cores(3, 0, down) + both_cores(0, 1, side)
    feats = load_feats(None, own_pieces + pieces)
    far, down_side, up_side, tiles, feats = lax.optimization_barrier(
        (far, down_side, up_side, tiles, feats)
    )
    thirds, at = [], 0
    for n, array, perm in zip(
        THIRDS, (up_side, down_side, far), (FROM_UP, FROM_DOWN, FROM_SIDE)
    ):
        thirds.append(send(array[at : at + n], perm))
        at += n
    feats = load_feats(
        feats, both_cores(2, 0, far) + both_cores(3, 1, down_side) + both_cores(1, 1, up_side)
    )
    thirds, feats = lax.optimization_barrier((thirds, feats))
    starts = (0, THIRDS[0], THIRDS[0] + THIRDS[1])
    feats = load_feats(feats, sum((both_cores(2, 1, a, at) for at, a in zip(starts, thirds)), []))
    sends = other_half(plan, tiles, feats)
    arrived = {}
    for away in (4, 3, 5, 2, 6, 1, 7, 0):
        arrived[away] = lax.ppermute(sends[away], "col", X_FLIP)
    own = own_half(plan, tiles, feats)
    half = TPD // 2
    plus, minus = hop(4, plan, own, arrived[4], (), (), ((0, half), (half, half)))
    plus, minus = lax.ppermute(plus, "col", Z_PLUS), lax.ppermute(minus, "col", Z_MINUS)
    for step, (a, b) in enumerate(((3, 5), (2, 6), (1, 7))):
        at_a, at_b = ((0,), (half,)) if step == 0 else ((0,), (0,))
        (plus,) = hop(a, plan, own, arrived[a], (plus,), at_a, ((0, TPD),))
        plus = lax.ppermute(plus, "col", Z_PLUS)
        (minus,) = hop(b, plan, own, arrived[b], (minus,), at_b, ((0, TPD),))
        minus = lax.ppermute(minus, "col", Z_MINUS)
    return last(plan, own, arrived[0], plus, minus, weight, out_bias.reshape(1, -1))


def solution(mesh):
    return jax.shard_map(
        on_device,
        mesh=mesh,
        in_specs=(
            P(("row", "col"), None),
            P("row", "col", None, None, None),
            P("row", "col", None),
            P("row", "col", None),
            P("row", "col"),
            P(),
            P(),
        ),
        out_specs=P(("row", "col"), None),
        check_vma=False,
    )
```

time: 470 us -> 130 us (0.28)
  waiting for transfers between devices: 347 us -> 60.2 us
  other arithmetic: 55.6 us -> 0.69 us
  starting transfers between devices: 0.04 us -> 47.4 us
  local copies, waits for them, and re-layouts: 37.3 us -> 4.64 us
  matrix products: 15.8 us -> 0 us
  Pallas kernels: 0 us -> 14.5 us
  between operations: 14.1 us -> 0.92 us
    reduce_scatter x1 -> x0, waiting for transfers between devices: 287 us -> none  [on_device(): lax.psum_scatter(partial_value.reshape(-1, feat_width), 'col', scatter_di...]
    ppermute x0 -> x36, waiting for transfers between devices: none -> 60.2 us  [the longest x8 24.2 us: on_device(): arrived[away] = lax.ppermute(sends[away], 'col', X_FLIP)]
    all_gather x1 -> x0, waiting for transfers between devices: 58.8 us -> none  [on_device(): gathered = lax.all_gather(node_feats, 'row', axis=0, tiled=True)]
    scatter-add x1 -> x0, other arithmetic: 54.2 us -> none  [on_device(): partial_value = partial_value.at[dest_ids].add(products)]
    ppermute x0 -> x36, starting transfers between devices: none -> 47.4 us  [the longest x19 16.4 us: send(): return lax.ppermute(array, 'row', perm)]
    select_n x1 -> x0, local copies, waits for them, and re-layouts: 17.4 us -> none  [on_device(): products = jnp.where(is_live[:, None, None], products, 0.0)]
    dot_general x2 -> x0, matrix products: 15.8 us -> none  [the longest x1 13.2 us: on_device(): jnp.einsum('kij,kjf->kif', tile_set, blocks[source_ids], preferred_elemen...]
    pallas_call x0 -> x15, Pallas kernels: none -> 14.5 us  [the longest x7 6.36 us: hop(): call(functools.partial(hop_kernel, away, pass_at, cuts), f'hop_{away}', o...]
  transfers between devices with their start and end apart: 2 -> 36, of which waited for: 2 -> 17; matrix products, arithmetic and copies ran while one was open for 0% -> 1% of each run, Pallas kernels for 0% -> 8%
where the time goes in v2:
time: 130 us; the launch traced here: 128 us
  waiting for transfers between devices  60.2 us (46%)
  starting transfers between devices  47.4 us (36%)
  Pallas kernels  14.5 us (11%)
  local copies, waits for them, and re-layouts  4.64 us (4%)
    ppermute x8, waiting for transfers between devices, on_device(): arrived[away] = lax.ppermute(sends[away], 'col', X_FLIP)  24.2 us
    ppermute x19, waiting for transfers between devices, send(): return lax.ppermute(array, 'row', perm)  17.8 us
    ppermute x19, starting transfers between devices, send(): return lax.ppermute(array, 'row', perm)  16.4 us
    ppermute x8, starting transfers between devices, on_device(): arrived[away] = lax.ppermute(sends[away], 'col', X_FLIP)  13.8 us
    ppermute x1, waiting for transfers between devices, on_device(): partner_dest = lax.ppermute(dest, 'col', X_FLIP)  8.28 us
    ppermute x3, starting transfers between devices, on_device(): minus = lax.ppermute(minus, 'col', Z_MINUS)  8.19 us
    pallas_call x7, Pallas kernels, hop(): call(functools.partial(hop_kernel, away, pass_at, cuts), f'hop_{away}', o...  6.36 us
    ppermute x1, starting transfers between devices, on_device(): lax.ppermute(minus, 'col', Z_MINUS)  6.32 us
  transfers between devices with their start and end apart: 36, of which 17 were waited for; matrix products, arithmetic and copies ran while one was open for 1% of the time, Pallas kernels for 8%

profile of v2, /device:TPU:1, one launch (start us, length us, event | category | flops | bytes accessed | tf_op | source)
XLA Modules:
  0.0 128.3 jit_solution(14876145249017845896)
XLA Ops:
  0.0 3.6 %collective-permute-start = (bf16[2048,128]{1,0:T(8,128)(2,1)}, bf16[2048,128]{1,0:T(8,128)(2,1)S(1)}, u32[]{:S(2)}, u32[]{:S(2)}) collective-permute-start(bf16[2048,128]{1,0:T(8,128)(2,1)} %refs_0_.1), channel_id=1, source_target_pairs={{0,192},{16,208},{32,224},{48,240},{64,0},{80,16},{96,32},{112,48}... | collective-permute-start | bytes 1572872 | tf_op jit(solution)/shard_map/ppermute | solution.py:290
  3.6 1.2 collective-permute-start.2
  4.8 1.2 collective-permute-start.7
  6.7 0.7 compare_select_fusion.dest
  7.4 2.5 %collective-permute-start.3 = (s32[1,256]{1,0:T(1,128)S(1)}, s32[1,256]{1,0:T(1,128)S(1)}, u32[]{:S(2)}, u32[]{:S(2)}) collective-permute-start(s32[1,256]{1,0:T(1,128)S(1)} %compare_select_fusion.dest), channel_id=1, source_target_pairs={{0,1},{1,0},{2,3},{3,2},{4,5},{5,4},{6,7},{7,6},{8,9},{9,8},{10,11... | collective-permute-start | bytes 3080 | tf_op jit(solution)/shard_map/ppermute | solution.py:305
  9.8 0.1 stack.23.where
  9.9 8.3 %collective-permute-done.3.partner_dest = s32[1,256]{1,0:T(1,128)S(1)} collective-permute-done((s32[1,256]{1,0:T(1,128)S(1)}, s32[1,256]{1,0:T(1,128)S(1)}, u32[]{:S(2)}, u32[]{:S(2)}) %collective-permute-start.3) | collective-permute-done | bytes 1056 | tf_op jit(solution)/shard_map/ppermute | solution.py:305
  18.2 0.7 copy-done.4
  18.9 1.1 plan.1
  19.9 2.2 %collective-permute-start.10 = (bf16[2048,128]{1,0:T(8,128)(2,1)S(1)}, bf16[2048,128]{1,0:T(8,128)(2,1)S(1)}, u32[]{:S(2)}, u32[]{:S(2)}) collective-permute-start(bf16[2048,128]{1,0:T(8,128)(2,1)S(1)} %collective-permute-done.2.refs_6_), channel_id=1, source_target_pairs={{0,16},{16,0},{32,48},{48,32},{64,80},{80,64},{96,112},{112,96},{1... | collective-permute-start | bytes 1572872 | tf_op jit(solution)/shard_map/ppermute | solution.py:290
  22.2 0.1 collective-permute-start.8
  22.3 2.7 %collective-permute-start.4 = (bf16[2048,128]{1,0:T(8,128)(2,1)S(1)}, bf16[2048,128]{1,0:T(8,128)(2,1)S(1)}, u32[]{:S(2)}, u32[]{:S(2)}) collective-permute-start(bf16[2048,128]{1,0:T(8,128)(2,1)S(1)} %collective-permute-done.refs_2_), channel_id=1, source_target_pairs={{0,192},{16,208},{32,224},{48,240},{64,0},{80,16},{96,32},{112,48}... | collective-permute-start | bytes 1572872 | tf_op jit(solution)/shard_map/ppermute | solution.py:290
  25.0 0.7 collective-permute-start.9
  25.7 0.1 collective-permute-start.6
  25.8 3.4 %copy-done = bf16[1,1,256,128,128]{4,3,2,1,0:T(8,128)(2,1)S(1)} copy-done((bf16[1,1,256,128,128]{4,3,2,1,0:T(8,128)(2,1)S(1)}, bf16[1,1,256,128,128]{4,3,2,1,0:T(8,128)(2,1)}, u32[]{:S(2)}) %copy-start) | copy-done | bytes 8388632
  29.2 0.6 load_tiles.1.tiles
  29.8 0.4 copy-done.1
  30.2 0.3 load_feats.3.refs_0_
  30.5 5.4 %collective-permute-done.4.refs_1_ = bf16[2048,128]{1,0:T(8,128)(2,1)S(1)} collective-permute-done((bf16[2048,128]{1,0:T(8,128)(2,1)S(1)}, bf16[2048,128]{1,0:T(8,128)(2,1)S(1)}, u32[]{:S(2)}, u32[]{:S(2)}) %collective-permute-start.4) | collective-permute-done | bytes 524320 | tf_op jit(solution)/shard_map/ppermute | solution.py:290
  35.9 4.6 %collective-permute-done.5.refs_3_ = bf16[2048,128]{1,0:T(8,128)(2,1)S(1)} collective-permute-done((bf16[2048,128]{1,0:T(8,128)(2,1)S(1)}, bf16[2048,128]{1,0:T(8,128)(2,1)S(1)}, u32[]{:S(2)}, u32[]{:S(2)}) %collective-permute-start.5) | collective-permute-done | bytes 524320 | tf_op jit(solution)/shard_map/ppermute | solution.py:290
  40.4 0.8 collective-permute-start.14
  41.2 0.5 collective-permute-start.16
  41.8 1.5 %collective-permute-start.11 = (bf16[688,128]{1,0:T(8,128)(2,1)S(1)}, bf16[688,128]{1,0:T(8,128)(2,1)S(1)}, u32[]{:S(2)}, u32[]{:S(2)}) collective-permute-start(bf16[688,128]{1,0:T(8,128)(2,1)S(1)} %slice.9), channel_id=1, source_target_pairs={{0,192},{16,208},{32,224},{48,240},{64,0},{80,16},{96,32},{112,48}... | collective-permute-start | bytes 528392 | tf_op jit(solution)/shard_map/ppermute | solution.py:290
  43.3 0.1 collective-permute-start.13
  43.5 0.7 collective-permute-done.16.refs_6_
  44.3 0.2 load_feats.4.refs_0_
  44.5 4.3 %collective-permute-done.13.refs_5_ = bf16[672,128]{1,0:T(8,128)(2,1)S(1)} collective-permute-done((bf16[672,128]{1,0:T(8,128)(2,1)S(1)}, bf16[672,128]{1,0:T(8,128)(2,1)S(1)}, u32[]{:S(2)}, u32[]{:S(2)}) %collective-permute-start.13) | collective-permute-done | bytes 172064 | tf_op jit(solution)/shard_map/ppermute | solution.py:290
  48.8 1.5 %collective-permute-done.12.refs_3_ = bf16[688,128]{1,0:T(8,128)(2,1)S(1)} collective-permute-done((bf16[688,128]{1,0:T(8,128)(2,1)S(1)}, bf16[688,128]{1,0:T(8,128)(2,1)S(1)}, u32[]{:S(2)}, u32[]{:S(2)}) %collective-permute-start.12) | collective-permute-done | bytes 176160 | tf_op jit(solution)/shard_map/ppermute | solution.py:290
  50.3 1.1 collective-permute-start.17
  51.4 0.5 collective-permute-start.19
  51.9 1.1 collective-permute-done.19.refs_6_
  53.1 1.7 %other_half.1 = (bf16[8,128,128]{2,1,0:T(8,128)(2,1)S(1)}, bf16[8,128,128]{2,1,0:T(8,128)(2,1)S(1)}, bf16[8,128,128]{2,1,0:T(8,128)(2,1)S(1)}, bf16[8,128,128]{2...) custom-call(s32[8,384]{1,0:T(8,128)S(1)} %plan.1, ...), custom_call_target="tpu_custom_call" | custom-call | tf_op jit(solution)/shard_map/other_half/pallas_call | solution.py:218
  54.8 2.9 %collective-permute-start.24 = (bf16[8,128,128]{2,1,0:T(8,128)(2,1)S(1)}, bf16[8,128,128]{2,1,0:T(8,128)(2,1)S(1)}, u32[]{:S(2)}, u32[]{:S(2)}) collective-permute-start(bf16[8,128,128]{2,1,0:T(8,128)(2,1)S(1)} %get-tuple-element.45), channel_id=1, source_target_pairs={{0,1},{1,0},{2,3},{3,2},{4,5},{5,4},{6,7},{7,6},{8,9},{9,8},{10,11... | collective-permute-start | bytes 786440 | tf_op jit(solution)/shard_map/ppermute | solution.py:332
  57.8 2.0 %own_half.1.own = f32[129,128,128]{2,1,0:T(8,128)S(1)} custom-call(s32[8,384]{1,0:T(8,128)S(1)} %plan.1, bf16[256,128,128]{2,1,0:T(8,128)(2,1)S(1)} %load_tiles.1.tiles, bf16[32768,128]{1,0:T(8,128)(2,1)S(1)} %load_feats.5.feats), custom_call_target="tpu_custom_call" | custom-call | tf_op jit(solution)/shard_map/own_half/pallas_call | solution.py:234
  59.8 2.1 %collective-permute-start.31 = (bf16[8,128,128]{2,1,0:T(8,128)(2,1)S(1)}, bf16[8,128,128]{2,1,0:T(8,128)(2,1)S(1)}, u32[]{:S(2)}, u32[]{:S(2)}) collective-permute-start(bf16[8,128,128]{2,1,0:T(8,128)(2,1)S(1)} %get-tuple-element.49), channel_id=1, source_target_pairs={{0,1},{1,0},{2,3},{3,2},{4,5},{5,4},{6,7},{7,6},{8,9},{9,8},{10,11... | collective-permute-start | bytes 786440 | tf_op jit(solution)/shard_map/ppermute | solution.py:332
  61.9 1.7 %collective-permute-done.24.arrived = bf16[8,128,128]{2,1,0:T(8,128)(2,1)S(1)} collective-permute-done((bf16[8,128,128]{2,1,0:T(8,128)(2,1)S(1)}, bf16[8,128,128]{2,1,0:T(8,128)(2,1)S(1)}, u32[]{:S(2)}, u32[]{:S(2)}) %collective-permute-start.24) | collective-permute-done | bytes 262176 | tf_op jit(solution)/shard_map/ppermute | solution.py:332
  63.7 0.9 hop_4.1
  64.5 6.3 %collective-permute-start.32 = (bf16[8,128,128]{2,1,0:T(8,128)(2,1)S(1)}, bf16[8,128,128]{2,1,0:T(8,128)(2,1)S(1)}, u32[]{:S(2)}, u32[]{:S(2)}) collective-permute-start(bf16[8,128,128]{2,1,0:T(8,128)(2,1)S(1)} %get-tuple-element.50), channel_id=1, source_target_pairs={{0,14},{1,15},{2,0},{3,1},{4,2},{5,3},{6,4},{7,5},{8,6},{9,7},{10,... | collective-permute-start | bytes 786440 | tf_op jit(solution)/shard_map/ppermute | solution.py:336
  70.9 2.6 %collective-permute-start.23 = (bf16[8,128,128]{2,1,0:T(8,128)(2,1)S(1)}, bf16[8,128,128]{2,1,0:T(8,128)(2,1)S(1)}, u32[]{:S(2)}, u32[]{:S(2)}) collective-permute-start(bf16[8,128,128]{2,1,0:T(8,128)(2,1)S(1)} %get-tuple-element.44), channel_id=1, source_target_pairs={{0,1},{1,0},{2,3},{3,2},{4,5},{5,4},{6,7},{7,6},{8,9},{9,8},{10,11... | collective-permute-start | bytes 786440 | tf_op jit(solution)/shard_map/ppermute | solution.py:332
  73.5 1.5 %collective-permute-done.32.refs_0_ = bf16[8,128,128]{2,1,0:T(8,128)(2,1)S(1)} collective-permute-done((bf16[8,128,128]{2,1,0:T(8,128)(2,1)S(1)}, bf16[8,128,128]{2,1,0:T(8,128)(2,1)S(1)}, u32[]{:S(2)}, u32[]{:S(2)}) %collective-permute-start.32) | collective-permute-done | bytes 262176 | tf_op jit(solution)/shard_map/ppermute | solution.py:336
  75.0 0.9 hop_5.1
  75.9 3.5 %collective-permute-start.33 = (bf16[16,128,128]{2,1,0:T(8,128)(2,1)S(1)}, bf16[16,128,128]{2,1,0:T(8,128)(2,1)S(1)}, u32[]{:S(2)}, u32[]{:S(2)}) collective-permute-start(bf16[16,128,128]{2,1,0:T(8,128)(2,1)S(1)} %hop_5.1), channel_id=1, source_target_pairs={{0,14},{1,15},{2,0},{3,1},{4,2},{5,3},{6,4},{7,5},{8,6},{9,7},{10,... | collective-permute-start | bytes 1572872 | tf_op jit(solution)/shard_map/ppermute | solution.py:342
  79.4 3.0 %collective-permute-done.25.refs_0_ = bf16[8,128,128]{2,1,0:T(8,128)(2,1)S(1)} collective-permute-done((bf16[8,128,128]{2,1,0:T(8,128)(2,1)S(1)}, bf16[8,128,128]{2,1,0:T(8,128)(2,1)S(1)}, u32[]{:S(2)}, u32[]{:S(2)}) %collective-permute-start.25) | collective-permute-done | bytes 262176 | tf_op jit(solution)/shard_map/ppermute | solution.py:336
  82.4 0.9 hop_3.1
  83.3 0.1 collective-permute-start.26
  83.3 0.4 collective-permute-start.30
  83.7 2.7 %collective-permute-start.22 = (bf16[8,128,128]{2,1,0:T(8,128)(2,1)S(1)}, bf16[8,128,128]{2,1,0:T(8,128)(2,1)S(1)}, u32[]{:S(2)}, u32[]{:S(2)}) collective-permute-start(bf16[8,128,128]{2,1,0:T(8,128)(2,1)S(1)} %get-tuple-element.43), channel_id=1, source_target_pairs={{0,1},{1,0},{2,3},{3,2},{4,5},{5,4},{6,7},{7,6},{8,9},{9,8},{10,11... | collective-permute-start | bytes 786440 | tf_op jit(solution)/shard_map/ppermute | solution.py:332
  86.4 6.0 %collective-permute-done.30.arrived = bf16[8,128,128]{2,1,0:T(8,128)(2,1)S(1)} collective-permute-done((bf16[8,128,128]{2,1,0:T(8,128)(2,1)S(1)}, bf16[8,128,128]{2,1,0:T(8,128)(2,1)S(1)}, u32[]{:S(2)}, u32[]{:S(2)}) %collective-permute-start.30) | collective-permute-done | bytes 262176 | tf_op jit(solution)/shard_map/ppermute | solution.py:332
  92.4 0.9 hop_6.1
  93.4 2.3 %collective-permute-start.34 = (bf16[16,128,128]{2,1,0:T(8,128)(2,1)S(1)}, bf16[16,128,128]{2,1,0:T(8,128)(2,1)S(1)}, u32[]{:S(2)}, u32[]{:S(2)}) collective-permute-start(bf16[16,128,128]{2,1,0:T(8,128)(2,1)S(1)} %hop_6.1), channel_id=1, source_target_pairs={{0,14},{1,15},{2,0},{3,1},{4,2},{5,3},{6,4},{7,5},{8,6},{9,7},{10,... | collective-permute-start | bytes 1572872 | tf_op jit(solution)/shard_map/ppermute | solution.py:342
  95.7 2.3 %collective-permute-done.22.arrived = bf16[8,128,128]{2,1,0:T(8,128)(2,1)S(1)} collective-permute-done((bf16[8,128,128]{2,1,0:T(8,128)(2,1)S(1)}, bf16[8,128,128]{2,1,0:T(8,128)(2,1)S(1)}, u32[]{:S(2)}, u32[]{:S(2)}) %collective-permute-start.22) | collective-permute-done | bytes 262176 | tf_op jit(solution)/shard_map/ppermute | solution.py:332
  98.0 0.9 hop_2.1
  99.0 0.1 collective-permute-start.27
  99.1 0.1 collective-permute-start.29
  99.2 2.9 %collective-permute-start.21 = (bf16[8,128,128]{2,1,0:T(8,128)(2,1)S(1)}, bf16[8,128,128]{2,1,0:T(8,128)(2,1)S(1)}, u32[]{:S(2)}, u32[]{:S(2)}) collective-permute-start(bf16[8,128,128]{2,1,0:T(8,128)(2,1)S(1)} %get-tuple-element.42), channel_id=1, source_target_pairs={{0,1},{1,0},{2,3},{3,2},{4,5},{5,4},{6,7},{7,6},{8,9},{9,8},{10,11... | collective-permute-start | bytes 786440 | tf_op jit(solution)/shard_map/ppermute | solution.py:332
  102.1 5.1 %collective-permute-done.29.arrived = bf16[8,128,128]{2,1,0:T(8,128)(2,1)S(1)} collective-permute-done((bf16[8,128,128]{2,1,0:T(8,128)(2,1)S(1)}, bf16[8,128,128]{2,1,0:T(8,128)(2,1)S(1)}, u32[]{:S(2)}, u32[]{:S(2)}) %collective-permute-start.29) | collective-permute-done | bytes 262176 | tf_op jit(solution)/shard_map/ppermute | solution.py:332
  107.2 0.9 hop_7.1
  108.2 2.4 %collective-permute-start.35 = (bf16[16,128,128]{2,1,0:T(8,128)(2,1)S(1)}, bf16[16,128,128]{2,1,0:T(8,128)(2,1)S(1)}, u32[]{:S(2)}, u32[]{:S(2)}) collective-permute-start(bf16[16,128,128]{2,1,0:T(8,128)(2,1)S(1)} %hop_7.1), channel_id=1, source_target_pairs={{0,14},{1,15},{2,0},{3,1},{4,2},{5,3},{6,4},{7,5},{8,6},{9,7},{10,... | collective-permute-start | bytes 1572872 | tf_op jit(solution)/shard_map/ppermute | solution.py:342
  110.5 2.3 %collective-permute-done.21.arrived = bf16[8,128,128]{2,1,0:T(8,128)(2,1)S(1)} collective-permute-done((bf16[8,128,128]{2,1,0:T(8,128)(2,1)S(1)}, bf16[8,128,128]{2,1,0:T(8,128)(2,1)S(1)}, u32[]{:S(2)}, u32[]{:S(2)}) %collective-permute-start.21) | collective-permute-done | bytes 262176 | tf_op jit(solution)/shard_map/ppermute | solution.py:332
  112.9 0.9 hop_1.1
  113.9 0.1 collective-permute-start.20
  114.0 6.7 %collective-permute-done.20.arrived = bf16[8,128,128]{2,1,0:T(8,128)(2,1)S(1)} collective-permute-done((bf16[8,128,128]{2,1,0:T(8,128)(2,1)S(1)}, bf16[8,128,128]{2,1,0:T(8,128)(2,1)S(1)}, u32[]{:S(2)}, u32[]{:S(2)}) %collective-permute-start.20) | collective-permute-done | bytes 262176 | tf_op jit(solution)/shard_map/ppermute | solution.py:332
  120.7 5.4 %collective-permute-done.28.passed_a = bf16[16,128,128]{2,1,0:T(8,128)(2,1)S(1)} collective-permute-done((bf16[16,128,128]{2,1,0:T(8,128)(2,1)S(1)}, bf16[16,128,128]{2,1,0:T(8,128)(2,1)S(1)}, u32[]{:S(2)}, u32[]{:S(2)}) %collective-permute-start.28) | collective-permute-done | bytes 524320 | tf_op jit(solution)/shard_map/ppermute | solution.py:340
  126.1 2.3 %last.1 = bf16[2048,256]{1,0:T(8,128)(2,1)} custom-call(s32[8,384]{1,0:T(8,128)S(1)} %plan.1, f32[129,128,128]{2,1,0:T(8,128)S(1)} %own_half.1.own, bf16[8,128,128]{2,1,0:T(8,128)(2,1)S(1)} %collective-permute-done.20.arrived, bf16[16,128,128]{2,1,0:T(8,128)(2,1)S(1)} %collective-permute-done.28.passed_a, ...), custom_call_target="tpu_custom_call" | custom-call | tf_op jit(solution)/shard_map/last/pallas_call | solution.py:280
  (38 shorter events, 0.3 us)
Async XLA Ops:
  0.0 19.9 %collective-permute-start = (bf16[2048,128]{1,0:T(8,128)(2,1)}, bf16[2048,128]{1,0:T(8,128)(2,1)S(1)}, u32[]{:S(2)}, u32[]{:S(2)}) collective-permute-start(bf16[2048,128]{1,0:T(8,128)(2,1)} %refs_0_.1), channel_id=1, source_target_pairs={{0,192},{16,208},{32,224},{48,240},{64,0},{80,16},{96,32},{112,48}... | collective-permute-start | bytes 1572872 | tf_op jit(solution)/shard_map/ppermute | solution.py:290
  3.6 16.4 %collective-permute-start.1 = (bf16[2048,128]{1,0:T(8,128)(2,1)}, bf16[2048,128]{1,0:T(8,128)(2,1)S(1)}, u32[]{:S(2)}, u32[]{:S(2)}) collective-permute-start(bf16[2048,128]{1,0:T(8,128)(2,1)} %refs_0_.1), channel_id=1, source_target_pairs={{0,64},{16,80},{32,96},{48,112},{64,128},{80,144},{96,160},{112,17... | collective-permute-start | bytes 1572872 | tf_op jit(solution)/shard_map/ppermute | solution.py:290
  3.6 16.4 %collective-permute-start.2 = (bf16[2048,128]{1,0:T(8,128)(2,1)}, bf16[2048,128]{1,0:T(8,128)(2,1)S(1)}, u32[]{:S(2)}, u32[]{:S(2)}) collective-permute-start(bf16[2048,128]{1,0:T(8,128)(2,1)} %refs_0_.1), channel_id=1, source_target_pairs={{0,32},{16,48},{32,0},{48,16},{64,96},{80,112},{96,64},{112,80},{1... | collective-permute-start | bytes 1572872 | tf_op jit(solution)/shard_map/ppermute | solution.py:290
  4.8 20.9 %collective-permute-start.7 = (bf16[2048,128]{1,0:T(8,128)(2,1)}, bf16[2048,128]{1,0:T(8,128)(2,1)S(1)}, u32[]{:S(2)}, u32[]{:S(2)}) collective-permute-start(bf16[2048,128]{1,0:T(8,128)(2,1)} %refs_0_.1), channel_id=1, source_target_pairs={{0,16},{16,0},{32,48},{48,32},{64,80},{80,64},{96,112},{112,96},{1... | collective-permute-start | bytes 1572872 | tf_op jit(solution)/shard_map/ppermute | solution.py:290
  7.4 10.8 %collective-permute-start.3 = (s32[1,256]{1,0:T(1,128)S(1)}, s32[1,256]{1,0:T(1,128)S(1)}, u32[]{:S(2)}, u32[]{:S(2)}) collective-permute-start(s32[1,256]{1,0:T(1,128)S(1)} %compare_select_fusion.dest), channel_id=1, source_target_pairs={{0,1},{1,0},{2,3},{3,2},{4,5},{5,4},{6,7},{7,6},{8,9},{9,8},{10,11... | collective-permute-start | bytes 3080 | tf_op jit(solution)/shard_map/ppermute | solution.py:305
  18.2 0.7 copy-start.4
  19.9 5.7 %collective-permute-start.10 = (bf16[2048,128]{1,0:T(8,128)(2,1)S(1)}, bf16[2048,128]{1,0:T(8,128)(2,1)S(1)}, u32[]{:S(2)}, u32[]{:S(2)}) collective-permute-start(bf16[2048,128]{1,0:T(8,128)(2,1)S(1)} %collective-permute-done.2.refs_6_), channel_id=1, source_target_pairs={{0,16},{16,0},{32,48},{48,32},{64,80},{80,64},{96,112},{112,96},{1... | collective-permute-start | bytes 1572872 | tf_op jit(solution)/shard_map/ppermute | solution.py:290
  22.2 7.5 %collective-permute-start.8 = (bf16[2048,128]{1,0:T(8,128)(2,1)S(1)}, bf16[2048,128]{1,0:T(8,128)(2,1)S(1)}, u32[]{:S(2)}, u32[]{:S(2)}) collective-permute-start(bf16[2048,128]{1,0:T(8,128)(2,1)S(1)} %collective-permute-done.refs_2_), channel_id=1, source_target_pairs={{0,16},{16,0},{32,48},{48,32},{64,80},{80,64},{96,112},{112,96},{1... | collective-permute-start | bytes 1572872 | tf_op jit(solution)/shard_map/ppermute | solution.py:290
  22.3 13.6 %collective-permute-start.4 = (bf16[2048,128]{1,0:T(8,128)(2,1)S(1)}, bf16[2048,128]{1,0:T(8,128)(2,1)S(1)}, u32[]{:S(2)}, u32[]{:S(2)}) collective-permute-start(bf16[2048,128]{1,0:T(8,128)(2,1)S(1)} %collective-permute-done.refs_2_), channel_id=1, source_target_pairs={{0,192},{16,208},{32,224},{48,240},{64,0},{80,16},{96,32},{112,48}... | collective-permute-start | bytes 1572872 | tf_op jit(solution)/shard_map/ppermute | solution.py:290
  25.0 4.8 %collective-permute-start.9 = (bf16[2048,128]{1,0:T(8,128)(2,1)S(1)}, bf16[2048,128]{1,0:T(8,128)(2,1)S(1)}, u32[]{:S(2)}, u32[]{:S(2)}) collective-permute-start(bf16[2048,128]{1,0:T(8,128)(2,1)S(1)} %collective-permute-done.1.refs_4_), channel_id=1, source_target_pairs={{0,16},{16,0},{32,48},{48,32},{64,80},{80,64},{96,112},{112,96},{1... | collective-permute-start | bytes 1572872 | tf_op jit(solution)/shard_map/ppermute | solution.py:290
  25.7 14.8 %collective-permute-start.5 = (bf16[2048,128]{1,0:T(8,128)(2,1)S(1)}, bf16[2048,128]{1,0:T(8,128)(2,1)S(1)}, u32[]{:S(2)}, u32[]{:S(2)}) collective-permute-start(bf16[2048,128]{1,0:T(8,128)(2,1)S(1)} %collective-permute-done.2.refs_6_), channel_id=1, source_target_pairs={{0,64},{16,80},{32,96},{48,112},{64,128},{80,144},{96,160},{112,17... | collective-permute-start | bytes 1572872 | tf_op jit(solution)/shard_map/ppermute | solution.py:290
  25.7 14.8 %collective-permute-start.6 = (bf16[2048,128]{1,0:T(8,128)(2,1)S(1)}, bf16[2048,128]{1,0:T(8,128)(2,1)S(1)}, u32[]{:S(2)}, u32[]{:S(2)}) collective-permute-start(bf16[2048,128]{1,0:T(8,128)(2,1)S(1)} %collective-permute-done.refs_2_), channel_id=1, source_target_pairs={{0,32},{16,48},{32,0},{48,16},{64,96},{80,112},{96,64},{112,80},{1... | collective-permute-start | bytes 1572872 | tf_op jit(solution)/shard_map/ppermute | solution.py:290
  25.8 3.4 %copy-start = (bf16[1,1,256,128,128]{4,3,2,1,0:T(8,128)(2,1)S(1)}, bf16[1,1,256,128,128]{4,3,2,1,0:T(8,128)(2,1)}, u32[]{:S(2)}) copy-start(bf16[1,1,256,128,128]{4,3,2,1,0:T(8,128)(2,1)} %param.8) | copy-start | bytes 25165828
  29.2 1.0 copy-start.1
  40.4 2.9 %collective-permute-start.14 = (bf16[2048,128]{1,0:T(8,128)(2,1)S(1)}, bf16[2048,128]{1,0:T(8,128)(2,1)S(1)}, u32[]{:S(2)}, u32[]{:S(2)}) collective-permute-start(bf16[2048,128]{1,0:T(8,128)(2,1)S(1)} %collective-permute-done.4.refs_1_), channel_id=1, source_target_pairs={{0,16},{16,0},{32,48},{48,32},{64,80},{80,64},{96,112},{112,96},{1... | collective-permute-start | bytes 1572872 | tf_op jit(solution)/shard_map/ppermute | solution.py:290
  41.2 2.3 %collective-permute-start.15 = (bf16[2048,128]{1,0:T(8,128)(2,1)S(1)}, bf16[2048,128]{1,0:T(8,128)(2,1)S(1)}, u32[]{:S(2)}, u32[]{:S(2)}) collective-permute-start(bf16[2048,128]{1,0:T(8,128)(2,1)S(1)} %collective-permute-done.5.refs_3_), channel_id=1, source_target_pairs={{0,16},{16,0},{32,48},{48,32},{64,80},{80,64},{96,112},{112,96},{1... | collective-permute-start | bytes 1572872 | tf_op jit(solution)/shard_map/ppermute | solution.py:290
  41.2 3.0 %collective-permute-start.16 = (bf16[2048,128]{1,0:T(8,128)(2,1)S(1)}, bf16[2048,128]{1,0:T(8,128)(2,1)S(1)}, u32[]{:S(2)}, u32[]{:S(2)}) collective-permute-start(bf16[2048,128]{1,0:T(8,128)(2,1)S(1)} %collective-permute-done.6.refs_5_), channel_id=1, source_target_pairs={{0,16},{16,0},{32,48},{48,32},{64,80},{80,64},{96,112},{112,96},{1... | collective-permute-start | bytes 1572872 | tf_op jit(solution)/shard_map/ppermute | solution.py:290
  41.8 7.0 %collective-permute-start.11 = (bf16[688,128]{1,0:T(8,128)(2,1)S(1)}, bf16[688,128]{1,0:T(8,128)(2,1)S(1)}, u32[]{:S(2)}, u32[]{:S(2)}) collective-permute-start(bf16[688,128]{1,0:T(8,128)(2,1)S(1)} %slice.9), channel_id=1, source_target_pairs={{0,192},{16,208},{32,224},{48,240},{64,0},{80,16},{96,32},{112,48}... | collective-permute-start | bytes 528392 | tf_op jit(solution)/shard_map/ppermute | solution.py:290
  43.3 7.0 %collective-permute-start.12 = (bf16[688,128]{1,0:T(8,128)(2,1)S(1)}, bf16[688,128]{1,0:T(8,128)(2,1)S(1)}, u32[]{:S(2)}, u32[]{:S(2)}) collective-permute-start(bf16[688,128]{1,0:T(8,128)(2,1)S(1)} %slice.10), channel_id=1, source_target_pairs={{0,64},{16,80},{32,96},{48,112},{64,128},{80,144},{96,160},{112,17... | collective-permute-start | bytes 528392 | tf_op jit(solution)/shard_map/ppermute | solution.py:290
  43.3 5.5 %collective-permute-start.13 = (bf16[672,128]{1,0:T(8,128)(2,1)S(1)}, bf16[672,128]{1,0:T(8,128)(2,1)S(1)}, u32[]{:S(2)}, u32[]{:S(2)}) collective-permute-start(bf16[672,128]{1,0:T(8,128)(2,1)S(1)} %slice.11), channel_id=1, source_target_pairs={{0,32},{16,48},{32,0},{48,16},{64,96},{80,112},{96,64},{112,80},{1... | collective-permute-start | bytes 516104 | tf_op jit(solution)/shard_map/ppermute | solution.py:290
  50.3 2.8 %collective-permute-start.17 = (bf16[688,128]{1,0:T(8,128)(2,1)S(1)}, bf16[688,128]{1,0:T(8,128)(2,1)S(1)}, u32[]{:S(2)}, u32[]{:S(2)}) collective-permute-start(bf16[688,128]{1,0:T(8,128)(2,1)S(1)} %collective-permute-done.11.refs_1_), channel_id=1, source_target_pairs={{0,16},{16,0},{32,48},{48,32},{64,80},{80,64},{96,112},{112,96},{1... | collective-permute-start | bytes 528392 | tf_op jit(solution)/shard_map/ppermute | solution.py:290
  51.4 1.7 %collective-permute-start.18 = (bf16[688,128]{1,0:T(8,128)(2,1)S(1)}, bf16[688,128]{1,0:T(8,128)(2,1)S(1)}, u32[]{:S(2)}, u32[]{:S(2)}) collective-permute-start(bf16[688,128]{1,0:T(8,128)(2,1)S(1)} %collective-permute-done.12.refs_3_), channel_id=1, source_target_pairs={{0,16},{16,0},{32,48},{48,32},{64,80},{80,64},{96,112},{112,96},{1... | collective-permute-start | bytes 528392 | tf_op jit(solution)/shard_map/ppermute | solution.py:290
  51.4 1.7 %collective-permute-start.19 = (bf16[672,128]{1,0:T(8,128)(2,1)S(1)}, bf16[672,128]{1,0:T(8,128)(2,1)S(1)}, u32[]{:S(2)}, u32[]{:S(2)}) collective-permute-start(bf16[672,128]{1,0:T(8,128)(2,1)S(1)} %collective-permute-done.13.refs_5_), channel_id=1, source_target_pairs={{0,16},{16,0},{32,48},{48,32},{64,80},{80,64},{96,112},{112,96},{1... | collective-permute-start | bytes 516104 | tf_op jit(solution)/shard_map/ppermute | solution.py:290
  54.8 8.8 %collective-permute-start.24 = (bf16[8,128,128]{2,1,0:T(8,128)(2,1)S(1)}, bf16[8,128,128]{2,1,0:T(8,128)(2,1)S(1)}, u32[]{:S(2)}, u32[]{:S(2)}) collective-permute-start(bf16[8,128,128]{2,1,0:T(8,128)(2,1)S(1)} %get-tuple-element.45), channel_id=1, source_target_pairs={{0,1},{1,0},{2,3},{3,2},{4,5},{5,4},{6,7},{7,6},{8,9},{9,8},{10,11... | collective-permute-start | bytes 786440 | tf_op jit(solution)/shard_map/ppermute | solution.py:332
  59.8 13.6 %collective-permute-start.31 = (bf16[8,128,128]{2,1,0:T(8,128)(2,1)S(1)}, bf16[8,128,128]{2,1,0:T(8,128)(2,1)S(1)}, u32[]{:S(2)}, u32[]{:S(2)}) collective-permute-start(bf16[8,128,128]{2,1,0:T(8,128)(2,1)S(1)} %get-tuple-element.49), channel_id=1, source_target_pairs={{0,1},{1,0},{2,3},{3,2},{4,5},{5,4},{6,7},{7,6},{8,9},{9,8},{10,11... | collective-permute-start | bytes 786440 | tf_op jit(solution)/shard_map/ppermute | solution.py:332
  64.5 10.4 %collective-permute-start.32 = (bf16[8,128,128]{2,1,0:T(8,128)(2,1)S(1)}, bf16[8,128,128]{2,1,0:T(8,128)(2,1)S(1)}, u32[]{:S(2)}, u32[]{:S(2)}) collective-permute-start(bf16[8,128,128]{2,1,0:T(8,128)(2,1)S(1)} %get-tuple-element.50), channel_id=1, source_target_pairs={{0,14},{1,15},{2,0},{3,1},{4,2},{5,3},{6,4},{7,5},{8,6},{9,7},{10,... | collective-permute-start | bytes 786440 | tf_op jit(solution)/shard_map/ppermute | solution.py:336
  70.9 8.5 %collective-permute-start.23 = (bf16[8,128,128]{2,1,0:T(8,128)(2,1)S(1)}, bf16[8,128,128]{2,1,0:T(8,128)(2,1)S(1)}, u32[]{:S(2)}, u32[]{:S(2)}) collective-permute-start(bf16[8,128,128]{2,1,0:T(8,128)(2,1)S(1)} %get-tuple-element.44), channel_id=1, source_target_pairs={{0,1},{1,0},{2,3},{3,2},{4,5},{5,4},{6,7},{7,6},{8,9},{9,8},{10,11... | collective-permute-start | bytes 786440 | tf_op jit(solution)/shard_map/ppermute | solution.py:332
  73.5 8.9 %collective-permute-start.25 = (bf16[8,128,128]{2,1,0:T(8,128)(2,1)S(1)}, bf16[8,128,128]{2,1,0:T(8,128)(2,1)S(1)}, u32[]{:S(2)}, u32[]{:S(2)}) collective-permute-start(bf16[8,128,128]{2,1,0:T(8,128)(2,1)S(1)} %get-tuple-element.46), channel_id=1, source_target_pairs={{0,2},{1,3},{2,4},{3,5},{4,6},{5,7},{6,8},{7,9},{8,10},{9,11},{10,... | collective-permute-start | bytes 786440 | tf_op jit(solution)/shard_map/ppermute | solution.py:336
  75.9 16.6 %collective-permute-start.33 = (bf16[16,128,128]{2,1,0:T(8,128)(2,1)S(1)}, bf16[16,128,128]{2,1,0:T(8,128)(2,1)S(1)}, u32[]{:S(2)}, u32[]{:S(2)}) collective-permute-start(bf16[16,128,128]{2,1,0:T(8,128)(2,1)S(1)} %hop_5.1), channel_id=1, source_target_pairs={{0,14},{1,15},{2,0},{3,1},{4,2},{5,3},{6,4},{7,5},{8,6},{9,7},{10,... | collective-permute-start | bytes 1572872 | tf_op jit(solution)/shard_map/ppermute | solution.py:342
  83.3 14.8 %collective-permute-start.26 = (bf16[16,128,128]{2,1,0:T(8,128)(2,1)S(1)}, bf16[16,128,128]{2,1,0:T(8,128)(2,1)S(1)}, u32[]{:S(2)}, u32[]{:S(2)}) collective-permute-start(bf16[16,128,128]{2,1,0:T(8,128)(2,1)S(1)} %hop_3.1), channel_id=1, source_target_pairs={{0,2},{1,3},{2,4},{3,5},{4,6},{5,7},{6,8},{7,9},{8,10},{9,11},{10,... | collective-permute-start | bytes 1572872 | tf_op jit(solution)/shard_map/ppermute | solution.py:340
  83.3 9.1 %collective-permute-start.30 = (bf16[8,128,128]{2,1,0:T(8,128)(2,1)S(1)}, bf16[8,128,128]{2,1,0:T(8,128)(2,1)S(1)}, u32[]{:S(2)}, u32[]{:S(2)}) collective-permute-start(bf16[8,128,128]{2,1,0:T(8,128)(2,1)S(1)} %get-tuple-element.48), channel_id=1, source_target_pairs={{0,1},{1,0},{2,3},{3,2},{4,5},{5,4},{6,7},{7,6},{8,9},{9,8},{10,11... | collective-permute-start | bytes 786440 | tf_op jit(solution)/shard_map/ppermute | solution.py:332
  83.7 14.3 %collective-permute-start.22 = (bf16[8,128,128]{2,1,0:T(8,128)(2,1)S(1)}, bf16[8,128,128]{2,1,0:T(8,128)(2,1)S(1)}, u32[]{:S(2)}, u32[]{:S(2)}) collective-permute-start(bf16[8,128,128]{2,1,0:T(8,128)(2,1)S(1)} %get-tuple-element.43), channel_id=1, source_target_pairs={{0,1},{1,0},{2,3},{3,2},{4,5},{5,4},{6,7},{7,6},{8,9},{9,8},{10,11... | collective-permute-start | bytes 786440 | tf_op jit(solution)/shard_map/ppermute | solution.py:332
  93.4 13.9 %collective-permute-start.34 = (bf16[16,128,128]{2,1,0:T(8,128)(2,1)S(1)}, bf16[16,128,128]{2,1,0:T(8,128)(2,1)S(1)}, u32[]{:S(2)}, u32[]{:S(2)}) collective-permute-start(bf16[16,128,128]{2,1,0:T(8,128)(2,1)S(1)} %hop_6.1), channel_id=1, source_target_pairs={{0,14},{1,15},{2,0},{3,1},{4,2},{5,3},{6,4},{7,5},{8,6},{9,7},{10,... | collective-permute-start | bytes 1572872 | tf_op jit(solution)/shard_map/ppermute | solution.py:342
  99.0 13.9 %collective-permute-start.27 = (bf16[16,128,128]{2,1,0:T(8,128)(2,1)S(1)}, bf16[16,128,128]{2,1,0:T(8,128)(2,1)S(1)}, u32[]{:S(2)}, u32[]{:S(2)}) collective-permute-start(bf16[16,128,128]{2,1,0:T(8,128)(2,1)S(1)} %hop_2.1), channel_id=1, source_target_pairs={{0,2},{1,3},{2,4},{3,5},{4,6},{5,7},{6,8},{7,9},{8,10},{9,11},{10,... | collective-permute-start | bytes 1572872 | tf_op jit(solution)/shard_map/ppermute | solution.py:340
  99.1 8.2 %collective-permute-start.29 = (bf16[8,128,128]{2,1,0:T(8,128)(2,1)S(1)}, bf16[8,128,128]{2,1,0:T(8,128)(2,1)S(1)}, u32[]{:S(2)}, u32[]{:S(2)}) collective-permute-start(bf16[8,128,128]{2,1,0:T(8,128)(2,1)S(1)} %get-tuple-element.47), channel_id=1, source_target_pairs={{0,1},{1,0},{2,3},{3,2},{4,5},{5,4},{6,7},{7,6},{8,9},{9,8},{10,11... | collective-permute-start | bytes 786440 | tf_op jit(solution)/shard_map/ppermute | solution.py:332
  99.2 26.9 %copy-start.2 = (bf16[128,256]{1,0:T(8,128)(2,1)S(1)}, bf16[128,256]{1,0:T(8,128)(2,1)}, u32[]{:S(2)}) copy-start(bf16[128,256]{1,0:T(8,128)(2,1)} %weight.1) | copy-start | bytes 196612
  99.2 26.9 %copy-start.3 = (f32[256]{0:T(256)S(1)}, f32[256]{0:T(256)}, u32[]{:S(2)}) copy-start(f32[256]{0:T(256)} %param.13) | copy-start | bytes 3076
  99.2 13.7 %collective-permute-start.21 = (bf16[8,128,128]{2,1,0:T(8,128)(2,1)S(1)}, bf16[8,128,128]{2,1,0:T(8,128)(2,1)S(1)}, u32[]{:S(2)}, u32[]{:S(2)}) collective-permute-start(bf16[8,128,128]{2,1,0:T(8,128)(2,1)S(1)} %get-tuple-element.42), channel_id=1, source_target_pairs={{0,1},{1,0},{2,3},{3,2},{4,5},{5,4},{6,7},{7,6},{8,9},{9,8},{10,11... | collective-permute-start | bytes 786440 | tf_op jit(solution)/shard_map/ppermute | solution.py:332
  108.2 12.5 %collective-permute-start.35 = (bf16[16,128,128]{2,1,0:T(8,128)(2,1)S(1)}, bf16[16,128,128]{2,1,0:T(8,128)(2,1)S(1)}, u32[]{:S(2)}, u32[]{:S(2)}) collective-permute-start(bf16[16,128,128]{2,1,0:T(8,128)(2,1)S(1)} %hop_7.1), channel_id=1, source_target_pairs={{0,14},{1,15},{2,0},{3,1},{4,2},{5,3},{6,4},{7,5},{8,6},{9,7},{10,... | collective-permute-start | bytes 1572872 | tf_op jit(solution)/shard_map/ppermute | solution.py:342
  113.8 12.3 %collective-permute-start.28 = (bf16[16,128,128]{2,1,0:T(8,128)(2,1)S(1)}, bf16[16,128,128]{2,1,0:T(8,128)(2,1)S(1)}, u32[]{:S(2)}, u32[]{:S(2)}) collective-permute-start(bf16[16,128,128]{2,1,0:T(8,128)(2,1)S(1)} %hop_1.1), channel_id=1, source_target_pairs={{0,2},{1,3},{2,4},{3,5},{4,6},{5,7},{6,8},{7,9},{8,10},{9,11},{10,... | collective-permute-start | bytes 1572872 | tf_op jit(solution)/shard_map/ppermute | solution.py:340
  113.9 6.8 %collective-permute-start.20 = (bf16[8,128,128]{2,1,0:T(8,128)(2,1)S(1)}, bf16[8,128,128]{2,1,0:T(8,128)(2,1)S(1)}, u32[]{:S(2)}, u32[]{:S(2)}) collective-permute-start(bf16[8,128,128]{2,1,0:T(8,128)(2,1)S(1)} %get-tuple-element.41), channel_id=1, source_target_pairs={{0,1},{1,0},{2,3},{3,2},{4,5},{5,4},{6,7},{7,6},{8,9},{9,8},{10,11... | collective-permute-start | bytes 786440 | tf_op jit(solution)/shard_map/ppermute | solution.py:332
